TPU v7x, 512 devices: a whole 4x4x16 slice. The times are simulated.
512 devices in a mesh: blk: 128 (over y, z, x_hi), head: 4 (over x_lo, core).
Axes of the slice: x: 4 (x_hi: 2, x_lo: 2; x = x_hi * 2 + x_lo), y: 4, z: 16, core: 2. Of those that a mesh axis runs over, the one named last changes fastest.
Arguments:
- query: bfloat16 [4, 512, 32, 512], P('head', 'blk'), may hold values from -8 to 8
- keyset: bfloat16 [4, 512, 32, 512], P('head', 'blk'), may hold values from -8 to 8
- values: bfloat16 [4, 512, 32, 512], P('head', 'blk'), may hold values from -6 to 6
- cotangent: bfloat16 [4, 512, 32, 512], P('head', 'blk'), may hold values from -24 to 24
- pair_norm: bfloat16 [128, 512, 512], P('head', 'blk'), may hold values from -6 to 6
- bias_weight: bfloat16 [128, 4], P('head'), may hold values from -0.5 to 0.5
Outputs:
- grad_query: bfloat16 [4, 512, 32, 512], P('head', 'blk')
- grad_key: bfloat16 [4, 512, 32, 512], P('head', 'blk')
- grad_value: bfloat16 [4, 512, 32, 512], P('head', 'blk')
- grad_pair: float32 [128, 512, 512], P('head', 'blk')
All inputs are finite; a program needn't handle non-finite values.
Results may differ from a plain program's by a relative error of at most 0.012.
Values may be sent and summed in bfloat16 or wider, within the bound.
No kernel may reach another device: no remote copies, remote signals or barrier semaphores. Data moves between devices by JAX's collectives and lax.ppermute only.
A program may use at most 64 MiB of HBM per device.

v0:
```python
import jax
import jax.numpy as jnp
from jax import lax
from jax.sharding import PartitionSpec as P

DH = 32
BLOCKS = 2
BLOCK_ROWS = 2


def attend_grads(query_rows, key_rows, value_rows, cotan_rows, bias_rows, groups):
    scale_factor = DH ** (-0.5)
    scores = (
        jnp.einsum("hrdj,hrdk->hrjk", query_rows, key_rows, preferred_element_type=jnp.float32)
        * scale_factor
    )
    scores = scores + bias_rows.astype(jnp.float32)[:, None]
    highest = jnp.max(scores, axis=-1, keepdims=True)
    weights = jnp.exp(scores - highest)
    probs = weights / jnp.sum(weights, axis=-1, keepdims=True)
    probs_low = probs.astype(jnp.bfloat16)
    output = jnp.einsum(
        "hrjk,hrdk->hrdj", probs_low, value_rows, preferred_element_type=jnp.float32
    )
    delta = jnp.sum(cotan_rows.astype(jnp.float32) * output, axis=2)
    dprobs = jnp.einsum(
        "hrdj,hrdk->hrjk", cotan_rows, value_rows, preferred_element_type=jnp.float32
    )
    dscores = probs * (dprobs - delta[..., None])
    dscores_low = dscores.astype(jnp.bfloat16)
    grad_q = (
        jnp.einsum("hrjk,hrdk->hrdj", dscores_low, key_rows, preferred_element_type=jnp.float32)
        * scale_factor
    )
    grad_k = (
        jnp.einsum("hrjk,hrdj->hrdk", dscores_low, query_rows, preferred_element_type=jnp.float32)
        * scale_factor
    )
    grad_v = jnp.einsum(
        "hrjk,hrdj->hrdk", probs_low, cotan_rows, preferred_element_type=jnp.float32
    )
    heads, rows, width, columns = dscores.shape
    grouped = jnp.sum(dscores.reshape(heads, groups, rows // groups, width, columns), axis=2)
    return (grad_q, grad_k, grad_v, grouped)


def shards(query, keyset, values, cotangent, pair_norm, bias_weight):
    partial_bias = jnp.einsum(
        "ch,cjk->hjk", bias_weight, pair_norm, preferred_element_type=jnp.float32
    )
    own_bias = lax.psum_scatter(partial_bias, "head", scatter_dimension=0, tiled=True).astype(
        jnp.bfloat16
    )
    local_heads = own_bias.shape[0]
    owned_rows = own_bias.shape[1]
    columns = own_bias.shape[2]
    full_bias = lax.all_gather(own_bias, "blk", axis=1, tiled=True)
    owned_grad = jnp.zeros((local_heads, owned_rows, columns), jnp.float32)
    query_parts, key_parts, value_parts = ([], [], [])
    for block_index in range(BLOCKS):
        lower = block_index * BLOCK_ROWS
        query_block = query[:, lower : lower + BLOCK_ROWS]
        key_block = keyset[:, lower : lower + BLOCK_ROWS]
        value_block = values[:, lower : lower + BLOCK_ROWS]
        cotan_block = cotangent[:, lower : lower + BLOCK_ROWS]
        grad_q, grad_k, grad_v, grouped = attend_grads(
            query_block, key_block, value_block, cotan_block, full_bias, 1
        )
        grad_block = grouped[:, 0]
        query_parts.append(grad_q.astype(jnp.bfloat16))
        key_parts.append(grad_k.astype(jnp.bfloat16))
        value_parts.append(grad_v.astype(jnp.bfloat16))
        owned_grad = owned_grad + lax.psum_scatter(
            grad_block, "blk", scatter_dimension=1, tiled=True
        )
    every_head = lax.all_gather(owned_grad, "head", axis=0, tiled=True)
    grad_pair = jnp.einsum(
        "ch,hjk->cjk", bias_weight.astype(jnp.float32), every_head, precision=lax.Precision.HIGHEST
    )
    return (
        jnp.concatenate(query_parts, axis=1),
        jnp.concatenate(key_parts, axis=1),
        jnp.concatenate(value_parts, axis=1),
        grad_pair,
    )


def solution(mesh):
    in_specs = (
        P("head", "blk", None, None),
        P("head", "blk", None, None),
        P("head", "blk", None, None),
        P("head", "blk", None, None),
        P("head", "blk", None),
        P("head", None),
    )
    out_specs = (
        P("head", "blk", None, None),
        P("head", "blk", None, None),
        P("head", "blk", None, None),
        P("head", "blk", None),
    )
    return jax.shard_map(shards, mesh=mesh, in_specs=in_specs, out_specs=out_specs, check_vma=False)
```

profile of v0, /device:TPU:1, one launch (start us, length us, event | category | flops | bytes accessed | tf_op | source)
XLA Modules:
  0.0 1777.7 jit_solution(1256500946489281412)
XLA Ops:
  7.2 0.0 copy-start
  7.2 0.0 copy-start.6
  7.2 0.0 copy-start.5
  7.2 0.0 all-reduce.4.cloned.1.call-start
  7.3 0.8 copy-done
  8.1 0.8 fusion.32
  8.9 16.4 all-reduce
  25.3 1.3 dynamic-slice
  26.6 0.7 dynamic-slice_convert_fusion
  27.2 307.3 %all_gather.6 = bf16[1,512,512]{2,0,1:T(2,128)(2,1)S(1)} all-gather(bf16[1,4,512]{2,0,1:T(2,128)(2,1)S(1)} %copy.25), channel_id=1, replica_groups=mesh['blk'=128,'head'=4] {'blk'}, dimensions={1}, use_global_device_ids=true | all-gather | bytes 528384 | tf_op jit(solution)/shard_map/all_gather | solution.py:57
  334.5 1.3 copy.51
  335.8 0.0 copy-done.6
  335.8 0.0 copy-done.5
  335.8 0.9 fusion.93
  336.7 2.2 fusion.98
  338.9 0.3 fusion.23
  339.2 0.6 copy-done.4
  339.8 0.1 copy-done.8
  339.9 0.3 fusion.10
  340.2 0.0 copy-start.1
  340.2 1.7 fusion.104
  341.9 0.0 copy-done.1
  341.9 0.3 fusion.22
  342.2 0.3 fusion.11
  342.5 1.7 fusion.103
  344.2 0.2 add_bitcast_fusion
  344.4 2.0 copy.37
  346.4 0.0 all-reduce.4.cloned.1.call-update
  346.4 1.0 fusion.13
  347.5 1.4 dynamic-slice.2
  349.5 0.0 copy-start.7
  349.5 0.4 fusion.12
  349.9 1.5 pad_maximum_fusion.2
  351.4 0.0 copy-done.2
  351.4 0.4 fusion.16
  351.8 0.0 copy-done.7
  351.9 0.0 copy-start.9
  351.9 0.3 fusion.14
  352.1 0.0 copy-done.3
  352.2 0.4 fusion.17
  352.6 0.3 fusion.15
  352.9 0.7 pad_maximum_fusion
  353.6 1318.8 %all-reduce.4.cloned.1.call-done = f32[1,512,512]{2,0,1:T(1,128)} async-done(((f32[1,512,512]{2,0,1:T(1,128)}), f32[1,512,512]{2,0,1:T(1,128)}) %all-reduce.4.cloned.1.call-update) | async-done | bytes 1048592
  1672.4 0.7 constant_dynamic-slice_fusion
  1673.1 96.6 %all_gather.7 = f32[4,4,512]{2,1,0:T(4,128)S(1)} all-gather(f32[1,4,512]{2,1,0:T(4,128)S(1)} %copy.38), channel_id=1, replica_groups=mesh['blk'=128,'head'=4] {'head'}, dimensions={0}, use_global_device_ids=true | all-gather | bytes 40960 | tf_op jit(solution)/shard_map/all_gather | solution.py:76
  1769.7 0.0 copy-done.9
  1769.7 0.3 convolution_bitcast_fusion
  1770.0 0.9 copy.40
  (7 shorter events, 0.0 us)
Async XLA Ops:
  7.2 0.9 copy-start
  7.2 328.6 %copy-start.6 = (bf16[1,4,32,512]{3,2,1,0:T(8,128)(2,1)S(1)}, bf16[1,4,32,512]{3,2,1,0:T(8,128)(2,1)}, u32[]{:S(2)}) copy-start(bf16[1,4,32,512]{3,2,1,0:T(8,128)(2,1)} %param.7) | copy-start | bytes 393220
  7.2 328.6 %copy-start.5 = (bf16[1,4,32,512]{3,2,1,0:T(8,128)(2,1)S(1)}, bf16[1,4,32,512]{3,2,1,0:T(8,128)(2,1)}, u32[]{:S(2)}) copy-start(bf16[1,4,32,512]{3,2,1,0:T(8,128)(2,1)} %param.6) | copy-start | bytes 393220
  7.2 1665.2 %all-reduce.4.cloned.1.call-start = ((), (), s32[]{:S(2)}) async-start(), calls=%async_computation | async-start | bytes 2097152
  338.9 0.9 copy-start.4
  338.9 1.0 copy-start.8
  340.2 1.7 copy-start.1
  346.4 5.0 copy-start.2
  347.5 4.7 copy-start.3
  349.5 2.4 copy-start.7
  351.9 1417.8 %copy-start.9 = (bf16[32,4]{0,1:T(4,128)(2,1)S(1)}, bf16[32,4]{0,1:T(4,128)(2,1)}, u32[]{:S(2)}) copy-start(bf16[32,4]{0,1:T(4,128)(2,1)} %param.11) | copy-start | bytes 772
Sparse Core Ops, SparseCore 0:
  346.6 1325.8 all-reduce.3
where the time goes:
time: 1780 us
  waiting for transfers between devices  1320 us (74%)
  blocking collectives  420 us (24%)
    unnamed x2, waiting for transfers between devices  1320 us
    all_gather x1, blocking collectives, shards(): full_bias = lax.all_gather(own_bias, 'blk', axis=1, tiled=True)  307 us
    all_gather x1, blocking collectives, shards(): every_head = lax.all_gather(owned_grad, 'head', axis=0, tiled=True)  96.6 us
  transfers between devices with their start and end apart: 1, of which 1 were waited for; matrix products, arithmetic and copies ran while one was open for 0% of the time, Pallas kernels for 0%

commit v1 on v0

v1 whole, which is shorter than its diff:
```python
import jax
import jax.numpy as jnp
from jax import lax
from jax.sharding import Mesh
from jax.sharding import PartitionSpec as P

DH = 32
BLK = ("y", "z", "xh")
HEAD = ("xl", "core")
RING = ("xh", "xl", "core")


def attend_grads(query_rows, key_rows, value_rows, cotan_rows, bias_rows):
    scale_factor = DH ** (-0.5)
    scores = (
        jnp.einsum("rdj,rdk->rjk", query_rows, key_rows, preferred_element_type=jnp.float32)
        * scale_factor
    )
    scores = scores + bias_rows.astype(jnp.float32)[None]
    highest = jnp.max(scores, axis=-1, keepdims=True)
    weights = jnp.exp(scores - highest)
    probs = weights / jnp.sum(weights, axis=-1, keepdims=True)
    probs_low = probs.astype(jnp.bfloat16)
    output = jnp.einsum("rjk,rdk->rdj", probs_low, value_rows, preferred_element_type=jnp.float32)
    delta = jnp.sum(cotan_rows.astype(jnp.float32) * output, axis=1)
    dprobs = jnp.einsum("rdj,rdk->rjk", cotan_rows, value_rows, preferred_element_type=jnp.float32)
    dscores = probs * (dprobs - delta[..., None])
    dscores_low = dscores.astype(jnp.bfloat16)
    grad_q = (
        jnp.einsum("rjk,rdk->rdj", dscores_low, key_rows, preferred_element_type=jnp.float32)
        * scale_factor
    )
    grad_k = (
        jnp.einsum("rjk,rdj->rdk", dscores_low, query_rows, preferred_element_type=jnp.float32)
        * scale_factor
    )
    grad_v = jnp.einsum("rjk,rdj->rdk", probs_low, cotan_rows, preferred_element_type=jnp.float32)
    return (
        grad_q.astype(jnp.bfloat16),
        grad_k.astype(jnp.bfloat16),
        grad_v.astype(jnp.bfloat16),
        jnp.sum(dscores, axis=0),
    )


def exchange(blocks, axes):
    return lax.all_to_all(blocks, axes, 0, 0, tiled=True)


def shards(query, keyset, values, cotangent, pair_norm, bias_weight):
    ny, nz, nx = lax.axis_size("y"), lax.axis_size("z"), lax.axis_size("xh")
    nh = lax.axis_size(HEAD)
    rows, width = pair_norm.shape[1:]
    partial = jnp.einsum("ch,cjk->hjk", bias_weight, pair_norm, preferred_element_type=jnp.float32)
    sent = jnp.broadcast_to(partial[None], (nx, nh, rows, width)).reshape(nx * nh, rows, width)
    parts = exchange(sent, RING).reshape(nx, nh, rows, width)
    own = jnp.sum(parts, axis=1).astype(jnp.bfloat16).reshape(nx * rows, width)
    plane = exchange(jnp.broadcast_to(own[None], (nz,) + own.shape), "z")
    plane = plane.reshape(nz * nx * rows, width)
    full = exchange(jnp.broadcast_to(plane[None], (ny,) + plane.shape), "y")
    full = full.reshape(ny * nz * nx * rows, width)

    grad_q, grad_k, grad_v, grad_bias = attend_grads(
        query[0], keyset[0], values[0], cotangent[0], full
    )

    low = grad_bias.astype(jnp.bfloat16).reshape(ny, nz * nx * rows, width)
    plane = jnp.sum(exchange(low, "y").astype(jnp.float32), axis=0).astype(jnp.bfloat16)
    plane = exchange(plane.reshape(nz, nx * rows, width), "z")
    own = jnp.sum(plane.astype(jnp.float32), axis=0).reshape(nx, 1, rows, width)
    sent = jnp.broadcast_to(own, (nx, nh, rows, width)).reshape(nx * nh, rows, width)
    every_head = jnp.sum(exchange(sent, RING).reshape(nx, nh, rows, width), axis=0)
    grad_pair = jnp.einsum(
        "ch,hjk->cjk", bias_weight.astype(jnp.float32), every_head, precision=lax.Precision.HIGHEST
    )
    return grad_q[None], grad_k[None], grad_v[None], grad_pair


def solution(mesh):
    fine = Mesh(mesh.devices.reshape(4, 16, 2, 2, 2), BLK + HEAD)
    four = P(HEAD, BLK, None, None)
    three = P(HEAD, BLK, None)
    return jax.shard_map(
        shards,
        mesh=fine,
        in_specs=(four, four, four, four, three, P(HEAD, None)),
        out_specs=(four, four, four, three),
        check_vma=False,
    )
```

time: 1780 us -> 105 us (0.06)
  waiting for transfers between devices: 1320 us -> 9.81 us
  blocking collectives: 420 us -> 57.4 us
    unnamed x2 -> x0, waiting for transfers between devices: 1320 us -> none
    all_gather x2 -> x0, blocking collectives: 404 us -> none  [the longest x1 307 us: shards(): full_bias = lax.all_gather(own_bias, 'blk', axis=1, tiled=True)]
    all_to_all x0 -> x4, blocking collectives: none -> 57.4 us  [exchange(): return lax.all_to_all(blocks, axes, 0, 0, tiled=True)]
  transfers between devices with their start and end apart: 1 -> 2, of which waited for: 1 -> 2; matrix products, arithmetic and copies ran while one was open for 0% -> 7% of each run, Pallas kernels for 0% -> 0%
where the time goes in v1:
time: 105 us; the launch traced here: 104 us
  blocking collectives  57.4 us (55%)
  starting transfers between devices  15.3 us (15%)
  matrix products  14.7 us (14%)
  waiting for transfers between devices  9.81 us (9%)
  local copies, waits for them, and re-layouts  3.29 us (3%)
  other arithmetic  3.25 us (3%)
    all_to_all x4, blocking collectives, exchange(): return lax.all_to_all(blocks, axes, 0, 0, tiled=True)  57.4 us
    all_to_all x2, starting transfers between devices, exchange(): return lax.all_to_all(blocks, axes, 0, 0, tiled=True)  15.3 us
    all_to_all x2, waiting for transfers between devices, exchange(): return lax.all_to_all(blocks, axes, 0, 0, tiled=True)  9.81 us
    sub x1, matrix products, attend_grads(): weights = jnp.exp(scores - highest)  3.43 us
    dot_general x1, matrix products, attend_grads(): jnp.einsum('rjk,rdj->rdk', dscores_low, query_rows, preferred_element_typ...  2.97 us
    convert_element_type x1, other arithmetic, attend_grads(): probs_low = probs.astype(jnp.bfloat16)  2.95 us
    dot_general x1, matrix products, attend_grads(): jnp.einsum('rjk,rdk->rdj', dscores_low, key_rows, preferred_element_type=...  2.68 us
    dot_general x1, matrix products, attend_grads(): jnp.einsum('rdj,rdk->rjk', cotan_rows, value_rows, preferred_element_type...  2.34 us
  transfers between devices with their start and end apart: 2, of which 2 were waited for; matrix products, arithmetic and copies ran while one was open for 7% of the time, Pallas kernels for 0%

profile of v1, /device:TPU:1, one launch (start us, length us, event | category | flops | bytes accessed | tf_op | source)
XLA Modules:
  0.0 104.5 jit_solution(6783997665653617288)
XLA Ops:
  0.6 0.0 copy-start
  0.6 0.0 copy-start.4
  0.7 0.0 copy-start.3
  0.7 1.1 %fusion.33 = f32[4,4,512]{2,0,1:T(4,128)S(1)} fusion(bf16[32,4,512]{2,1,0:T(4,128)(2,1)} %param.10, bf16[32,4]{0,1:T(4,128)(2,1)} %param.11), kind=kOutput, calls=%fused_computation.39 | convolution fusion | flops 524288 | bytes 164096 | tf_op jit(solution)/shard_map/ch,cjk->hjk/dot_general | solution.py:54
  1.8 14.1 %all_to_all.30 = f32[8,4,512]{2,1,0:T(4,128)S(1)} all-to-all(f32[8,4,512]{2,1,0:T(4,128)S(1)} %bitcast.91), channel_id=1, replica_groups=mesh['y'=4,'z'=16,'xh'=2,'xl'=2,'core'=2] {'xh','xl','core'}, dimensions={0} | all-to-all | bytes 131072 | tf_op jit(solution)/shard_map/all_to_all | solution.py:47
  16.0 23.1 %all_to_all.31 = bf16[16,8,512]{2,1,0:T(8,128)(2,1)S(1)} all-to-all(bf16[16,8,512]{2,1,0:T(8,128)(2,1)S(1)} %broadcast_in_dim.19), channel_id=1, replica_groups=mesh['y'=4,'z'=16,'xh'=2,'xl'=2,'core'=2] {'z'}, dimensions={0} | all-to-all | bytes 262144 | tf_op jit(solution)/shard_map/all_to_all | solution.py:47
  39.0 0.1 copy.76
  39.1 0.1 broadcast_in_dim.41
  39.2 10.9 %all_to_all.32 = bf16[4,128,512]{1,2,0:T(8,128)(2,1)S(1)} all-to-all(bf16[4,128,512]{1,2,0:T(8,128)(2,1)S(1)} %broadcast_in_dim.41), channel_id=1, replica_groups=mesh['y'=4,'z'=16,'xh'=2,'xl'=2,'core'=2] {'y'}, dimensions={0} | all-to-all | bytes 1048576 | tf_op jit(solution)/shard_map/all_to_all | solution.py:47
  50.1 0.2 copy.77
  50.4 0.2 bitcast_convert_fusion
  50.5 0.3 copy.78
  50.9 0.0 copy-done.4
  50.9 0.0 copy-done.3
  50.9 3.4 %fusion.39 = (f32[4,512]{1,0:T(4,128)S(1)}, f32[4,512,512]{1,2,0:T(8,128)}) fusion(f32[512,512]{0,1:T(8,128)S(1)} %copy.78, bf16[1,4,32,512]{3,2,1,0:T(8,128)(2,1)S(1)} %copy-done.4, bf16[1,4,32,512]{3,2,1,0:T(8,128)(2,1)S(1)} %copy-done.3), kind=kOutput, calls=%fused_computation.46 | convolution fusion | flops 71303680 | bytes 5513216 | tf_op jit(solution)/shard_map/sub | solution.py:21
  54.3 0.0 copy-start.2
  54.3 0.0 copy-start.1
  54.3 2.9 %fusion.4 = bf16[4,512,512]{1,2,0:T(8,128)(2,1)S(1)} fusion(f32[4,512,512]{1,2,0:T(8,128)} %get-tuple-element.33, f32[4,512]{1,0:T(4,128)S(1)} %get-tuple-element.32), kind=kLoop, calls=%fused_computation.8 | loop fusion | flops 2097152 | bytes 6299648 | tf_op jit(solution)/shard_map/convert_element_type | solution.py:23
  57.3 0.0 copy-done
  57.3 0.0 copy-done.2
  57.3 0.5 fusion.8
  57.8 0.1 copy-done.1
  57.8 2.3 %fusion.48 = (bf16[512,512]{0,1:T(8,128)(2,1)S(1)}, bf16[4,512,512]{1,2,0:T(8,128)(2,1)}) fusion(f32[4,512]{1,0:T(4,128)S(1)} %fusion.8, bf16[1,4,32,512]{3,2,1,0:T(8,128)(2,1)S(1)} %copy-done, bf16[1,4,32,512]{3,2,1,0:T(8,128)(2,1)S(1)} %copy-done.2, f32[4,512,512]{1,2,0:T(8,128)S(1)} %copy-done.1, f32[4,512]{1,0:T(4,128)S(1)} %get-tuple-element.32), kind=kOutput, calls=%fused_computation.47 | convolution fusion | flops 72089600 | bytes 7094272 | tf_op jit(solution)/shard_map/rdj,rdk->rjk/dot_general | solution.py:26
  60.2 0.1 copy_bitcast_fusion
  60.3 9.3 %all_to_all.33 = bf16[4,128,512]{1,2,0:T(8,128)(2,1)S(1)} all-to-all(bf16[4,128,512]{1,2,0:T(8,128)(2,1)S(1)} %copy_bitcast_fusion), channel_id=1, replica_groups=mesh['y'=4,'z'=16,'xh'=2,'xl'=2,'core'=2] {'y'}, dimensions={0} | all-to-all | bytes 1048576 | tf_op jit(solution)/shard_map/all_to_all | solution.py:47
  69.6 0.1 reduce_sum.70
  69.7 0.0 copy-start.5
  69.7 0.8 copy.86
  70.5 6.9 %all-to-all-start.4 = ((bf16[16,8,512]{2,1,0:T(8,128)(2,1)}), bf16[16,8,512]{2,1,0:T(8,128)(2,1)S(1)}, u32[]{:S(2)}, u32[]{:S(2)}) async-start(bf16[16,8,512]{2,1,0:T(8,128)(2,1)} %bitcast.16), calls=%async_computation.4 | async-start | bytes 262144 | tf_op jit(solution)/shard_map/all_to_all | solution.py:47
  77.4 1.4 %fusion.11 = bf16[1,4,32,512]{3,2,1,0:T(8,128)(2,1)} fusion(bf16[4,512,512]{1,2,0:T(8,128)(2,1)S(1)} %fusion.4, bf16[1,4,32,512]{3,2,1,0:T(8,128)(2,1)S(1)} %copy-done.2), kind=kOutput, calls=%fused_computation.20 | convolution fusion | flops 67174400 | bytes 2359296 | tf_op jit(solution)/shard_map/rjk,rdj->rdk/dot_general | solution.py:37
  78.7 3.0 %fusion.10 = bf16[1,4,32,512]{3,2,1,0:T(8,128)(2,1)} fusion(bf16[4,512,512]{1,2,0:T(8,128)(2,1)} %get-tuple-element.35, bf16[1,4,32,512]{3,2,1,0:T(8,128)(2,1)S(1)} %copy-done.3), kind=kOutput, calls=%fused_computation.19 | convolution fusion | flops 67239936 | bytes 2359296 | tf_op jit(solution)/shard_map/rjk,rdj->rdk/dot_general | solution.py:34
  81.7 7.6 %all-to-all-done.4 = bf16[16,8,512]{2,1,0:T(8,128)(2,1)S(1)} async-done(((bf16[16,8,512]{2,1,0:T(8,128)(2,1)}), bf16[16,8,512]{2,1,0:T(8,128)(2,1)S(1)}, u32[]{:S(2)}, u32[]{:S(2)}) %all-to-all-start.4) | async-done | bytes 131104 | tf_op jit(solution)/shard_map/all_to_all | solution.py:47
  89.4 0.6 broadcast_in_dim.46
  90.0 8.4 %all-to-all-start.5 = ((f32[8,4,512]{2,1,0:T(4,128)}), f32[8,4,512]{2,1,0:T(4,128)S(1)}, u32[]{:S(2)}, u32[]{:S(2)}) async-start(f32[8,4,512]{2,1,0:T(4,128)} %bitcast.17), calls=%async_computation.5 | async-start | bytes 131072 | tf_op jit(solution)/shard_map/all_to_all | solution.py:47
  98.4 2.7 %fusion.9 = bf16[1,4,32,512]{3,2,1,0:T(8,128)(2,1)} fusion(bf16[4,512,512]{1,2,0:T(8,128)(2,1)} %get-tuple-element.35, bf16[1,4,32,512]{3,2,1,0:T(8,128)(2,1)S(1)} %copy-done.4), kind=kOutput, calls=%fused_computation.18 | convolution fusion | flops 67239936 | bytes 2359296 | tf_op jit(solution)/shard_map/rjk,rdk->rdj/dot_general | solution.py:30
  101.1 2.2 %all-to-all-done.5 = f32[8,4,512]{2,1,0:T(4,128)S(1)} async-done(((f32[8,4,512]{2,1,0:T(4,128)}), f32[8,4,512]{2,1,0:T(4,128)S(1)}, u32[]{:S(2)}, u32[]{:S(2)}) %all-to-all-start.5) | async-done | bytes 65568 | tf_op jit(solution)/shard_map/all_to_all | solution.py:47
  103.3 0.0 copy-done.5
  103.3 0.3 convolution_bitcast_fusion.1
  103.6 0.9 copy.88
  (8 shorter events, 0.1 us)
Async XLA Ops:
  0.6 56.6 %copy-start = (bf16[1,4,32,512]{3,2,1,0:T(8,128)(2,1)S(1)}, bf16[1,4,32,512]{3,2,1,0:T(8,128)(2,1)}, u32[]{:S(2)}) copy-start(bf16[1,4,32,512]{3,2,1,0:T(8,128)(2,1)} %param.8) | copy-start | bytes 393220
  0.6 50.2 %copy-start.4 = (bf16[1,4,32,512]{3,2,1,0:T(8,128)(2,1)S(1)}, bf16[1,4,32,512]{3,2,1,0:T(8,128)(2,1)}, u32[]{:S(2)}) copy-start(bf16[1,4,32,512]{3,2,1,0:T(8,128)(2,1)} %param.7) | copy-start | bytes 393220
  0.7 50.2 %copy-start.3 = (bf16[1,4,32,512]{3,2,1,0:T(8,128)(2,1)S(1)}, bf16[1,4,32,512]{3,2,1,0:T(8,128)(2,1)}, u32[]{:S(2)}) copy-start(bf16[1,4,32,512]{3,2,1,0:T(8,128)(2,1)} %param.6) | copy-start | bytes 393220
  54.3 3.0 %copy-start.2 = (bf16[1,4,32,512]{3,2,1,0:T(8,128)(2,1)S(1)}, bf16[1,4,32,512]{3,2,1,0:T(8,128)(2,1)}, u32[]{:S(2)}) copy-start(bf16[1,4,32,512]{3,2,1,0:T(8,128)(2,1)} %param.9) | copy-start | bytes 393220
  54.3 3.5 %copy-start.1 = (f32[4,512,512]{1,2,0:T(8,128)S(1)}, f32[4,512,512]{1,2,0:T(8,128)}, u32[]{:S(2)}) copy-start(f32[4,512,512]{1,2,0:T(8,128)} %get-tuple-element.33) | copy-start | bytes 12582916
  69.7 33.6 %copy-start.5 = (bf16[32,4]{0,1:T(4,128)(2,1)S(1)}, bf16[32,4]{0,1:T(4,128)(2,1)}, u32[]{:S(2)}) copy-start(bf16[32,4]{0,1:T(4,128)(2,1)} %param.11) | copy-start | bytes 772
  70.5 18.9 %all-to-all-start.4 = ((bf16[16,8,512]{2,1,0:T(8,128)(2,1)}), bf16[16,8,512]{2,1,0:T(8,128)(2,1)S(1)}, u32[]{:S(2)}, u32[]{:S(2)}) async-start(bf16[16,8,512]{2,1,0:T(8,128)(2,1)} %bitcast.16), calls=%async_computation.4 | async-start | bytes 262144 | tf_op jit(solution)/shard_map/all_to_all | solution.py:47
  90.0 13.3 %all-to-all-start.5 = ((f32[8,4,512]{2,1,0:T(4,128)}), f32[8,4,512]{2,1,0:T(4,128)S(1)}, u32[]{:S(2)}, u32[]{:S(2)}) async-start(f32[8,4,512]{2,1,0:T(4,128)} %bitcast.17), calls=%async_computation.5 | async-start | bytes 131072 | tf_op jit(solution)/shard_map/all_to_all | solution.py:47

commit v2 on v1

v2 whole, which is shorter than its diff:
```python
import jax
import jax.numpy as jnp
from jax import lax
from jax.experimental import pallas as pl
from jax.experimental.pallas import tpu as pltpu
from jax.sharding import Mesh
from jax.sharding import PartitionSpec as P

DH = 32
BLK = ("y", "z", "xh")
HEAD = ("xl", "core")
RING = ("xh", "xl", "core")
TILE = 128
LIMIT = 48 * 1024 * 1024


def scores_kernel(query, keyset, values, cotangent, bias, total, probs_low, dscores_low):
    wide = bias[...].astype(jnp.float32)
    summed = None
    for row in range(query.shape[0]):
        scores = lax.dot_general(
            query[row], keyset[row], (((0,), (0,)), ((), ())), preferred_element_type=jnp.float32
        )
        scores = scores * DH ** (-0.5) + wide
        weights = jnp.exp(scores - jnp.max(scores, axis=-1, keepdims=True))
        probs = weights * (1.0 / jnp.sum(weights, axis=-1, keepdims=True))
        low = probs.astype(jnp.bfloat16)
        probs_low[row] = low
        dprobs = lax.dot_general(
            cotangent[row], values[row], (((0,), (0,)), ((), ())), preferred_element_type=jnp.float32
        )
        delta = jnp.sum(low.astype(jnp.float32) * dprobs, axis=-1, keepdims=True)
        dscores = probs * (dprobs - delta)
        dscores_low[row] = dscores.astype(jnp.bfloat16)
        summed = dscores if summed is None else summed + dscores
    total[...] = summed.astype(jnp.bfloat16)


def score_grads(query, keyset, values, cotangent, bias):
    rows, depth, width = query.shape
    block = pl.BlockSpec((rows, depth, TILE), lambda j: (0, 0, j))
    whole = pl.BlockSpec((rows, depth, width), lambda j: (0, 0, 0))
    flat = pl.BlockSpec((TILE, width), lambda j: (j, 0))
    tall = pl.BlockSpec((rows, TILE, width), lambda j: (0, j, 0))
    square = jax.ShapeDtypeStruct((rows, width, width), jnp.bfloat16)
    return pl.pallas_call(
        scores_kernel,
        grid=(width // TILE,),
        in_specs=[block, whole, whole, block, flat],
        out_specs=[flat, tall, tall],
        out_shape=[jax.ShapeDtypeStruct((width, width), jnp.bfloat16), square, square],
        compiler_params=pltpu.CompilerParams(vmem_limit_bytes=LIMIT),
        name="score_grads",
    )(query, keyset, values, cotangent, bias)


def inputs_kernel(query, keyset, cotangent, probs_low, dscores_low, grad_q, grad_k, grad_v):
    scale = DH ** (-0.5)
    dscores = dscores_low[...]
    grad_q[...] = (
        lax.dot_general(
            keyset[...], dscores, (((1,), (1,)), ((), ())), preferred_element_type=jnp.float32
        )
        * scale
    ).astype(jnp.bfloat16)
    grad_k[...] = (
        jnp.dot(query[...], dscores, preferred_element_type=jnp.float32) * scale
    ).astype(jnp.bfloat16)
    grad_v[...] = jnp.dot(
        cotangent[...], probs_low[...], preferred_element_type=jnp.float32
    ).astype(jnp.bfloat16)


def input_grads(query, keyset, cotangent, probs_low, dscores_low):
    rows, depth, width = query.shape
    thin = pl.BlockSpec((None, depth, width), lambda i: (i, 0, 0))
    square = pl.BlockSpec((None, width, width), lambda i: (i, 0, 0))
    shape = jax.ShapeDtypeStruct(query.shape, jnp.bfloat16)
    return pl.pallas_call(
        inputs_kernel,
        grid=(rows,),
        in_specs=[thin, thin, thin, square, square],
        out_specs=[thin, thin, thin],
        out_shape=[shape, shape, shape],
        compiler_params=pltpu.CompilerParams(vmem_limit_bytes=LIMIT),
        cost_estimate=pl.CostEstimate(
            flops=6 * rows * depth * width * width, bytes_accessed=8 << 20, transcendentals=0
        ),
        name="input_grads",
    )(query, keyset, cotangent, probs_low, dscores_low)


def exchange(blocks, axes):
    return lax.all_to_all(blocks, axes, 0, 0, tiled=True)


def shards(query, keyset, values, cotangent, pair_norm, bias_weight):
    ny, nz, nx = lax.axis_size("y"), lax.axis_size("z"), lax.axis_size("xh")
    nh = lax.axis_size(HEAD)
    rows, width = pair_norm.shape[1:]
    partial = jnp.einsum("ch,cjk->hjk", bias_weight, pair_norm, preferred_element_type=jnp.float32)
    sent = jnp.broadcast_to(partial[None], (nx, nh, rows, width)).reshape(nx * nh, rows, width)
    parts = exchange(sent, RING).reshape(nx, nh, rows, width)
    own = jnp.sum(parts, axis=1).astype(jnp.bfloat16).reshape(nx * rows, width)
    plane = exchange(jnp.broadcast_to(own[None], (nz,) + own.shape), "z")
    plane = plane.reshape(nz * nx * rows, width)
    full = exchange(jnp.broadcast_to(plane[None], (ny,) + plane.shape), "y")
    full = full.reshape(ny * nz * nx * rows, width)

    query, keyset, values, cotangent = query[0], keyset[0], values[0], cotangent[0]
    total, probs_low, dscores_low = score_grads(query, keyset, values, cotangent, full)
    grad_q, grad_k, grad_v = input_grads(query, keyset, cotangent, probs_low, dscores_low)

    plane = exchange(total.reshape(ny, nz * nx * rows, width), "y")
    plane = jnp.sum(plane.astype(jnp.float32), axis=0).astype(jnp.bfloat16)
    plane = exchange(plane.reshape(nz, nx * rows, width), "z")
    own = jnp.sum(plane.astype(jnp.float32), axis=0).reshape(nx, 1, rows, width)
    sent = jnp.broadcast_to(own, (nx, nh, rows, width)).reshape(nx * nh, rows, width)
    every_head = jnp.sum(exchange(sent, RING).reshape(nx, nh, rows, width), axis=0)
    grad_pair = jnp.einsum(
        "ch,hjk->cjk", bias_weight.astype(jnp.float32), every_head, precision=lax.Precision.HIGHEST
    )
    return grad_q[None], grad_k[None], grad_v[None], grad_pair


def solution(mesh):
    fine = Mesh(mesh.devices.reshape(4, 16, 2, 2, 2), BLK + HEAD)
    four = P(HEAD, BLK, None, None)
    three = P(HEAD, BLK, None)
    return jax.shard_map(
        shards,
        mesh=fine,
        in_specs=(four, four, four, four, three, P(HEAD, None)),
        out_specs=(four, four, four, three),
        check_vma=False,
    )
```

time: 105 us -> 99.3 us (0.946)
  blocking collectives: 57.4 us -> 76 us
  matrix products: 14.7 us -> 1.16 us
  waiting for transfers between devices: 9.81 us -> 0.7 us
  starting transfers between devices: 15.3 us -> 8.39 us
  Pallas kernels: 0 us -> 6.3 us
  other arithmetic: 3.25 us -> 0.14 us
  local copies, waits for them, and re-layouts: 3.29 us -> 5.43 us
    all_to_all x4 -> x5, blocking collectives: 57.4 us -> 76 us  [exchange(): return lax.all_to_all(blocks, axes, 0, 0, tiled=True)]
    dot_general x5 -> x0, matrix products: 9.82 us -> none  [the longest x1 2.97 us: attend_grads(): jnp.einsum('rjk,rdj->rdk', dscores_low, query_rows, preferred_element_typ...]
    all_to_all x2 -> x1, waiting for transfers between devices: 9.81 us -> 0.7 us  [exchange(): return lax.all_to_all(blocks, axes, 0, 0, tiled=True)]
    all_to_all x2 -> x1, starting transfers between devices: 15.3 us -> 8.39 us  [exchange(): return lax.all_to_all(blocks, axes, 0, 0, tiled=True)]
    pallas_call x0 -> x2, Pallas kernels: none -> 6.3 us  [the longest x1 3.73 us: score_grads(): pl.pallas_call(scores_kernel, grid=(width // TILE,), in_specs=[block, who...]
    unnamed x13 -> x17, local copies, waits for them, and re-layouts: 1 us -> 4.7 us
    sub x1 -> x0, matrix products: 3.43 us -> none  [attend_grads(): weights = jnp.exp(scores - highest)]
    convert_element_type x2 -> x0, other arithmetic: 3.1 us -> none  [the longest x1 2.95 us: attend_grads(): probs_low = probs.astype(jnp.bfloat16)]
  transfers between devices with their start and end apart: 2 -> 1, of which waited for: 2 -> 1; matrix products, arithmetic and copies ran while one was open for 7% -> 0% of each run, Pallas kernels for 0% -> 3%
where the time goes in v2:
time: 99.3 us; the launch traced here: 98.9 us
  blocking collectives  76 us (77%)
  starting transfers between devices  8.39 us (8%)
  Pallas kernels  6.3 us (6%)
  local copies, waits for them, and re-layouts  5.43 us (5%)
  matrix products  1.16 us (1%)
    all_to_all x5, blocking collectives, exchange(): return lax.all_to_all(blocks, axes, 0, 0, tiled=True)  76 us
    all_to_all x1, starting transfers between devices, exchange(): return lax.all_to_all(blocks, axes, 0, 0, tiled=True)  8.39 us
    unnamed x17, local copies, waits for them, and re-layouts  4.7 us
    pallas_call x1, Pallas kernels, score_grads(): pl.pallas_call(scores_kernel, grid=(width // TILE,), in_specs=[block, who...  3.73 us
    pallas_call x1, Pallas kernels, input_grads(): pl.pallas_call(inputs_kernel, grid=(rows,), in_specs=[thin, thin, thin, s...  2.57 us
  transfers between devices with their start and end apart: 1, of which 1 were waited for; matrix products, arithmetic and copies ran while one was open for 0% of the time, Pallas kernels for 3%

profile of v2, /device:TPU:1, one launch (start us, length us, event | category | flops | bytes accessed | tf_op | source)
XLA Modules:
  0.0 98.9 jit_solution(9538824011321867059)
XLA Ops:
  0.6 0.0 copy-start
  0.6 0.0 copy-start.5
  0.7 0.0 copy-start.6
  0.7 0.0 copy-start.4
  0.7 0.9 copy-done
  1.5 0.0 copy-start.3
  1.5 0.9 fusion
  2.4 14.1 %all_to_all.30 = f32[8,4,512]{2,1,0:T(4,128)S(1)} all-to-all(f32[8,4,512]{2,1,0:T(4,128)S(1)} %bitcast.35), channel_id=1, replica_groups=mesh['y'=4,'z'=16,'xh'=2,'xl'=2,'core'=2] {'xh','xl','core'}, dimensions={0} | all-to-all | bytes 131072 | tf_op jit(solution)/shard_map/all_to_all | solution.py:94
  16.6 23.1 %all_to_all.31 = bf16[16,8,512]{2,1,0:T(8,128)(2,1)S(1)} all-to-all(bf16[16,8,512]{2,1,0:T(8,128)(2,1)S(1)} %broadcast_in_dim.35), channel_id=1, replica_groups=mesh['y'=4,'z'=16,'xh'=2,'xl'=2,'core'=2] {'z'}, dimensions={0} | all-to-all | bytes 262144 | tf_op jit(solution)/shard_map/all_to_all | solution.py:94
  39.7 10.9 %all_to_all.32 = bf16[4,128,512]{2,1,0:T(8,128)(2,1)S(1)} all-to-all(bf16[4,128,512]{2,1,0:T(8,128)(2,1)S(1)} %broadcast_in_dim.37), channel_id=1, replica_groups=mesh['y'=4,'z'=16,'xh'=2,'xl'=2,'core'=2] {'y'}, dimensions={0} | all-to-all | bytes 1048576 | tf_op jit(solution)/shard_map/all_to_all | solution.py:94
  50.6 0.0 copy-done.5
  50.6 0.0 copy-done.6
  50.6 0.0 copy-done.4
  50.6 0.0 copy-done.3
  50.6 3.7 %score_grads.1 = (bf16[512,512]{1,0:T(8,128)(2,1)S(1)}, bf16[4,512,512]{2,1,0:T(8,128)(2,1)S(1)}, bf16[4,512,512]{2,1,0:T(8,128)(2,1)S(1)}) custom-call(bf16[4,32,512]{2,1,0:T(8,128)(2,1)S(1)} %bitcast.25, bf16[4,32,512]{2,1,0:T(8,128)(2,1)S(1)} %bitcast.27, bf16[4,32,512]{2,1,0:T(8,128)(2,1)S(1)} %bitcast.31, bf16[4,32,512]{2,1,0:T(8,128)(2,1)S(1)} %bitcast.29, ...), custom_call_target="tpu_custom_call" | custom-call | tf_op jit(solution)/shard_map/score_grads/pallas_call | solution.py:46
  54.4 0.0 copy-start.1
  54.4 1.3 %copy-done.1 = bf16[4,512,512]{2,1,0:T(8,128)(2,1)} copy-done((bf16[4,512,512]{2,1,0:T(8,128)(2,1)}, bf16[4,512,512]{2,1,0:T(8,128)(2,1)S(1)}, u32[]{:S(2)}) %copy-start.1) | copy-done | bytes 2097176
  55.7 9.3 %all_to_all.33 = bf16[4,128,512]{2,1,0:T(8,128)(2,1)S(1)} all-to-all(bf16[4,128,512]{2,1,0:T(8,128)(2,1)S(1)} %bitcast.24), channel_id=1, replica_groups=mesh['y'=4,'z'=16,'xh'=2,'xl'=2,'core'=2] {'y'}, dimensions={0} | all-to-all | bytes 1048576 | tf_op jit(solution)/shard_map/all_to_all | solution.py:94
  65.0 0.1 reduce_sum.40
  65.1 18.7 %all_to_all.34 = bf16[16,8,512]{2,1,0:T(8,128)(2,1)S(1)} all-to-all(bf16[16,8,512]{2,1,0:T(8,128)(2,1)S(1)} %bitcast.33), channel_id=1, replica_groups=mesh['y'=4,'z'=16,'xh'=2,'xl'=2,'core'=2] {'z'}, dimensions={0} | all-to-all | bytes 262144 | tf_op jit(solution)/shard_map/all_to_all | solution.py:94
  83.8 0.6 broadcast_in_dim.42
  84.4 8.4 %all-to-all-start.5 = ((f32[8,4,512]{2,1,0:T(4,128)}), f32[8,4,512]{2,1,0:T(4,128)S(1)}, u32[]{:S(2)}, u32[]{:S(2)}) async-start(f32[8,4,512]{2,1,0:T(4,128)} %bitcast.14), calls=%async_computation.5 | async-start | bytes 131072 | tf_op jit(solution)/shard_map/all_to_all | solution.py:94
  92.8 0.0 copy-start.2
  92.8 1.6 %copy-done.2 = bf16[4,512,512]{2,1,0:T(8,128)(2,1)S(1)} copy-done((bf16[4,512,512]{2,1,0:T(8,128)(2,1)S(1)}, bf16[4,512,512]{2,1,0:T(8,128)(2,1)}, u32[]{:S(2)}) %copy-start.2) | copy-done | bytes 2097176
  94.4 0.0 copy-start.7
  94.4 2.6 %input_grads.1 = (bf16[4,32,512]{2,1,0:T(8,128)(2,1)}, bf16[4,32,512]{2,1,0:T(8,128)(2,1)}, bf16[4,32,512]{2,1,0:T(8,128)(2,1)}) custom-call(bf16[4,32,512]{2,1,0:T(8,128)(2,1)S(1)} %bitcast.26, bf16[4,32,512]{2,1,0:T(8,128)(2,1)S(1)} %bitcast.28, bf16[4,32,512]{2,1,0:T(8,128)(2,1)S(1)} %bitcast.30, bf16[4,512,512]{2,1,0:T(8,128)(2,1)S(1)} %get-tuple-element.10.probs_low, ...), custom_call_target="tpu_custom_call" | custom-call | flops 201326592 | bytes 8388608 | tf_op jit(solution)/shard_map/input_grads/pallas_call | solution.py:79
  97.0 0.7 all-to-all-done.5
  97.7 0.0 copy-done.7
  97.7 0.3 convolution_bitcast_fusion
  98.0 0.9 copy.16
  (9 shorter events, 0.2 us)
Async XLA Ops:
  0.6 0.9 copy-start
  0.6 50.0 %copy-start.5 = (bf16[1,4,32,512]{3,2,1,0:T(8,128)(2,1)S(1)}, bf16[1,4,32,512]{3,2,1,0:T(8,128)(2,1)}, u32[]{:S(2)}) copy-start(bf16[1,4,32,512]{3,2,1,0:T(8,128)(2,1)} %param.9) | copy-start | bytes 393220
  0.7 50.0 %copy-start.6 = (bf16[1,4,32,512]{3,2,1,0:T(8,128)(2,1)S(1)}, bf16[1,4,32,512]{3,2,1,0:T(8,128)(2,1)}, u32[]{:S(2)}) copy-start(bf16[1,4,32,512]{3,2,1,0:T(8,128)(2,1)} %param.8) | copy-start | bytes 393220
  0.7 49.9 %copy-start.4 = (bf16[1,4,32,512]{3,2,1,0:T(8,128)(2,1)S(1)}, bf16[1,4,32,512]{3,2,1,0:T(8,128)(2,1)}, u32[]{:S(2)}) copy-start(bf16[1,4,32,512]{3,2,1,0:T(8,128)(2,1)} %param.7) | copy-start | bytes 393220
  1.5 49.1 %copy-start.3 = (bf16[1,4,32,512]{3,2,1,0:T(8,128)(2,1)S(1)}, bf16[1,4,32,512]{3,2,1,0:T(8,128)(2,1)}, u32[]{:S(2)}) copy-start(bf16[1,4,32,512]{3,2,1,0:T(8,128)(2,1)} %param.6) | copy-start | bytes 393220
  54.4 1.3 %copy-start.1 = (bf16[4,512,512]{2,1,0:T(8,128)(2,1)}, bf16[4,512,512]{2,1,0:T(8,128)(2,1)S(1)}, u32[]{:S(2)}) copy-start(bf16[4,512,512]{2,1,0:T(8,128)(2,1)S(1)} %get-tuple-element.11.dscores_low) | copy-start | bytes 6291460
  84.4 13.3 %all-to-all-start.5 = ((f32[8,4,512]{2,1,0:T(4,128)}), f32[8,4,512]{2,1,0:T(4,128)S(1)}, u32[]{:S(2)}, u32[]{:S(2)}) async-start(f32[8,4,512]{2,1,0:T(4,128)} %bitcast.14), calls=%async_computation.5 | async-start | bytes 131072 | tf_op jit(solution)/shard_map/all_to_all | solution.py:94
  92.8 1.6 %copy-start.2 = (bf16[4,512,512]{2,1,0:T(8,128)(2,1)S(1)}, bf16[4,512,512]{2,1,0:T(8,128)(2,1)}, u32[]{:S(2)}) copy-start(bf16[4,512,512]{2,1,0:T(8,128)(2,1)} %copy-done.1) | copy-start | bytes 6291460
  94.4 3.3 %copy-start.7 = (bf16[32,4]{0,1:T(4,128)(2,1)S(1)}, bf16[32,4]{0,1:T(4,128)(2,1)}, u32[]{:S(2)}) copy-start(bf16[32,4]{0,1:T(4,128)(2,1)} %param.11) | copy-start | bytes 772

commit v3 on v2

v3 whole, which is shorter than its diff:
```python
import math

import jax
import jax.numpy as jnp
from jax import lax
from jax.experimental import pallas as pl
from jax.experimental.pallas import tpu as pltpu
from jax.sharding import Mesh
from jax.sharding import PartitionSpec as P

DH = 32
BLK = ("y", "z", "xh")
HEAD = ("xl", "core")
PLANE = ("y", "xh")
LIMIT = 24 * 1024 * 1024
LOG2E = math.log2(math.e)
OUTER = (((0,), (0,)), ((), ()))


def first_half(shape):
    return lax.broadcasted_iota(jnp.int32, shape, 1) < shape[1] // 2


def interleave(low, high):
    half = first_half(low.shape)
    even = jnp.where(half, low, pltpu.roll(high, 4, 1))
    odd = jnp.where(half, pltpu.roll(low, 4, 1), high)
    return jnp.stack([even, odd], axis=1).reshape(-1, low.shape[-1])


def separate(rows):
    pairs = rows.reshape(-1, 2, 8, rows.shape[-1])
    even, odd = pairs[:, 0], pairs[:, 1]
    half = first_half(even.shape)
    low = jnp.where(half, even, pltpu.roll(odd, 4, 1))
    high = jnp.where(half, pltpu.roll(even, 4, 1), odd)
    return low.reshape(-1, rows.shape[-1]), high.reshape(-1, rows.shape[-1])


def bias_tile(bias):
    wide = bias[...].astype(jnp.float32) * LOG2E
    wide = wide.reshape(2, -1, 8, wide.shape[-1])
    return interleave(wide[0], wide[1])


def softmax_parts(query, keyset, wide):
    scores = lax.dot_general(query, keyset, OUTER, preferred_element_type=jnp.float32)
    scores = scores * (LOG2E * DH ** (-0.5)) + wide
    weights = jnp.exp2(scores - jnp.max(scores, axis=-1, keepdims=True))
    return weights, 1.0 / jnp.sum(weights, axis=-1, keepdims=True)


def sum_kernel(query, keyset, values, cotangent, bias, total):
    wide = bias_tile(bias)
    summed = None
    for row in range(query.shape[0]):
        weights, inverse = softmax_parts(query[row], keyset[row], wide)
        dprobs = lax.dot_general(
            cotangent[row], values[row], OUTER, preferred_element_type=jnp.float32
        )
        delta = jnp.sum(weights * dprobs, axis=-1, keepdims=True) * inverse
        dscores = (weights * inverse) * (dprobs - delta)
        summed = dscores if summed is None else summed + dscores
    low, high = separate(summed)
    total[0] = low.astype(jnp.bfloat16)
    total[1] = high.astype(jnp.bfloat16)


def inputs_kernel(query, keyset, values, cotangent, bias, grad_q, grad_k, grad_v, sum_k, sum_v):
    step = pl.program_id(0)
    wide = bias_tile(bias)

    @pl.when(step == 0)
    def _():
        sum_k[...] = jnp.zeros_like(sum_k)
        sum_v[...] = jnp.zeros_like(sum_v)

    for row in range(query.shape[0]):
        weights, inverse = softmax_parts(query[row], keyset[row], wide)
        probs = weights * inverse
        low = probs.astype(jnp.bfloat16)
        dprobs = lax.dot_general(
            cotangent[row], values[row], OUTER, preferred_element_type=jnp.float32
        )
        delta = jnp.sum(low.astype(jnp.float32) * dprobs, axis=-1, keepdims=True)
        dscores = (probs * (dprobs - delta)).astype(jnp.bfloat16)
        sum_k[row] += jnp.dot(query[row], dscores, preferred_element_type=jnp.float32)
        sum_v[row] += jnp.dot(cotangent[row], low, preferred_element_type=jnp.float32)
        turned = lax.dot_general(
            keyset[row], dscores, (((1,), (1,)), ((), ())), preferred_element_type=jnp.float32
        )
        grad_q[row] = (turned * DH ** (-0.5)).astype(jnp.bfloat16)

    @pl.when(step == pl.num_programs(0) - 1)
    def _():
        grad_k[...] = (sum_k[...] * DH ** (-0.5)).astype(jnp.bfloat16)
        grad_v[...] = sum_v[...].astype(jnp.bfloat16)


def specs(query, bias):
    rows, depth, width = query.shape
    tiles = bias.shape[0] // 2
    block = pl.BlockSpec((rows, depth, width // tiles), lambda j: (0, 0, j))
    whole = pl.BlockSpec((rows, depth, width), lambda j: (0, 0, 0))
    pair = pl.BlockSpec((2,) + bias.shape[1:], lambda j: (j, 0, 0))
    return tiles, block, whole, pair


def bias_sum(query, keyset, values, cotangent, bias):
    tiles, block, whole, pair = specs(query, bias)
    return pl.pallas_call(
        sum_kernel,
        grid=(tiles,),
        in_specs=[block, whole, whole, block, pair],
        out_specs=pair,
        out_shape=jax.ShapeDtypeStruct(bias.shape, jnp.bfloat16),
        compiler_params=pltpu.CompilerParams(vmem_limit_bytes=LIMIT),
        name="bias_sum",
    )(query, keyset, values, cotangent, bias)


def input_grads(query, keyset, values, cotangent, bias):
    tiles, block, whole, pair = specs(query, bias)
    rows, depth, width = query.shape
    shape = jax.ShapeDtypeStruct(query.shape, jnp.bfloat16)
    return pl.pallas_call(
        inputs_kernel,
        grid=(tiles,),
        in_specs=[block, whole, whole, block, pair],
        out_specs=[block, whole, whole],
        out_shape=[shape] * 3,
        scratch_shapes=[pltpu.VMEM(query.shape, jnp.float32)] * 2,
        compiler_params=pltpu.CompilerParams(vmem_limit_bytes=LIMIT),
        cost_estimate=pl.CostEstimate(
            flops=10 * rows * depth * width * width,
            bytes_accessed=1 << 20,
            transcendentals=rows * width * width,
        ),
        name="input_grads",
    )(query, keyset, values, cotangent, bias)


def pair_kernel(weight, every_head, grad_pair):
    cores, pairs = every_head.shape[:2]
    for head in range(pairs * cores):
        scale = weight[:, head : head + 1].astype(jnp.float32)[:, :, None]
        term = scale * every_head[head % cores, head // cores][None]
        if head == 0:
            grad_pair[...] = term
        else:
            grad_pair[...] += term


def pair_grad(weight, every_head):
    held = pl.BlockSpec(memory_space=pltpu.VMEM)
    return pl.pallas_call(
        pair_kernel,
        in_specs=[held, held],
        out_specs=held,
        out_shape=jax.ShapeDtypeStruct(weight.shape[:1] + every_head.shape[2:], jnp.float32),
        compiler_params=pltpu.CompilerParams(vmem_limit_bytes=LIMIT),
        name="pair_grad",
    )(weight, every_head)


def exchange(blocks, axes):
    return lax.all_to_all(blocks, axes, 0, 0, tiled=True)


def shards(query, keyset, values, cotangent, pair_norm, bias_weight):
    nz = lax.axis_size("z")
    planes = lax.axis_size(PLANE)
    rows, width = pair_norm.shape[1:]
    query, keyset, values, cotangent = query[0], keyset[0], values[0], cotangent[0]

    partial = jnp.einsum("ch,cjk->hjk", bias_weight, pair_norm, preferred_element_type=jnp.float32)
    own = jnp.sum(exchange(partial, HEAD), axis=0).astype(jnp.bfloat16)
    line = exchange(jnp.broadcast_to(own[None], (nz, rows, width)), "z").reshape(nz * rows, width)
    bias = exchange(jnp.broadcast_to(line[None], (planes,) + line.shape), PLANE)

    total = bias_sum(query, keyset, values, cotangent, bias)
    line = jnp.sum(exchange(total, PLANE).astype(jnp.float32), axis=0).astype(jnp.bfloat16)
    pairs = lax.axis_size("xl")
    line = jnp.broadcast_to(line.reshape(nz, 1, rows, width), (nz, pairs, rows, width))
    line = exchange(line.reshape(nz * pairs, rows, width), ("z", "xl"))
    grads = input_grads(query, keyset, values, cotangent, bias)
    line, *grads = lax.optimization_barrier((line, *grads))
    own = jnp.sum(line.astype(jnp.float32).reshape(nz, pairs, rows, width), axis=0)
    every_head = lax.all_gather(own, "core", axis=0)
    grad_pair = pair_grad(bias_weight, every_head)
    return grads[0][None], grads[1][None], grads[2][None], grad_pair


def solution(mesh):
    fine = Mesh(mesh.devices.reshape(4, 16, 2, 2, 2), BLK + HEAD)
    four = P(HEAD, BLK, None, None)
    three = P(HEAD, BLK, None)
    return jax.shard_map(
        shards,
        mesh=fine,
        in_specs=(four, four, four, four, three, P(HEAD, None)),
        out_specs=(four, four, four, three),
        check_vma=False,
    )
```

time: 99.3 us -> 93.4 us (0.941)
  blocking collectives: 76 us -> 67.6 us
  Pallas kernels: 6.3 us -> 13.7 us
  starting transfers between devices: 8.39 us -> 4.32 us
  local copies, waits for them, and re-layouts: 5.43 us -> 1.85 us
  waiting for transfers between devices: 0.7 us -> 3.9 us
    all_to_all x5 -> x4, blocking collectives: 76 us -> 60.5 us  [exchange(): return lax.all_to_all(blocks, axes, 0, 0, tiled=True)]
    pallas_call x2 -> x3, Pallas kernels: 6.3 us -> 13.7 us  [the longest x1 9.79 us: input_grads(): pl.pallas_call(inputs_kernel, grid=(tiles,), in_specs=[block, whole, whol...]
    all_gather x0 -> x1, blocking collectives: none -> 7.11 us  [shards(): every_head = lax.all_gather(own, 'core', axis=0)]
    all_to_all x1, starting transfers between devices: 8.39 us -> 4.32 us  [exchange(): return lax.all_to_all(blocks, axes, 0, 0, tiled=True)]
    unnamed x17 -> x13, local copies, waits for them, and re-layouts: 4.7 us -> 1.03 us
    all_to_all x1, waiting for transfers between devices: 0.7 us -> 3.9 us  [exchange(): return lax.all_to_all(blocks, axes, 0, 0, tiled=True)]
  transfers between devices with their start and end apart: 1 -> 1, of which waited for: 1 -> 1; matrix products, arithmetic and copies ran while one was open for 0% -> 0% of each run, Pallas kernels for 3% -> 11%
where the time goes in v3:
time: 93.4 us; the launch traced here: 93.1 us
  blocking collectives  67.6 us (72%)
  Pallas kernels  13.7 us (15%)
  starting transfers between devices  4.32 us (5%)
  waiting for transfers between devices  3.9 us (4%)
  local copies, waits for them, and re-layouts  1.85 us (2%)
    all_to_all x4, blocking collectives, exchange(): return lax.all_to_all(blocks, axes, 0, 0, tiled=True)  60.5 us
    pallas_call x1, Pallas kernels, input_grads(): pl.pallas_call(inputs_kernel, grid=(tiles,), in_specs=[block, whole, whol...  9.79 us
    all_gather x1, blocking collectives, shards(): every_head = lax.all_gather(own, 'core', axis=0)  7.11 us
    all_to_all x1, starting transfers between devices, exchange(): return lax.all_to_all(blocks, axes, 0, 0, tiled=True)  4.32 us
    all_to_all x1, waiting for transfers between devices, exchange(): return lax.all_to_all(blocks, axes, 0, 0, tiled=True)  3.9 us
    pallas_call x1, Pallas kernels, bias_sum(): pl.pallas_call(sum_kernel, grid=(tiles,), in_specs=[block, whole, whole,...  2.97 us
  transfers between devices with their start and end apart: 1, of which 1 were waited for; matrix products, arithmetic and copies ran while one was open for 0% of the time, Pallas kernels for 11%

profile of v3, /device:TPU:1, one launch (start us, length us, event | category | flops | bytes accessed | tf_op | source)
XLA Modules:
  0.0 93.1 jit_solution(10045882408212393972)
XLA Ops:
  0.6 0.0 copy-start
  0.6 0.9 copy-done
  1.5 0.8 fusion
  2.4 12.4 %all_to_all.25 = f32[4,4,512]{2,1,0:T(4,128)S(1)} all-to-all(f32[4,4,512]{2,1,0:T(4,128)S(1)} %copy.19), channel_id=1, replica_groups=mesh['y'=4,'z'=16,'xh'=2,'xl'=2,'core'=2] {'xl','core'}, dimensions={0} | all-to-all | bytes 65536 | tf_op jit(solution)/shard_map/all_to_all | solution.py:167
  14.8 21.1 %all_to_all.26 = bf16[16,4,512]{2,1,0:T(4,128)(2,1)S(1)} all-to-all(bf16[16,4,512]{2,1,0:T(4,128)(2,1)S(1)} %broadcast_in_dim.29), channel_id=1, replica_groups=mesh['y'=4,'z'=16,'xh'=2,'xl'=2,'core'=2] {'z'}, dimensions={0} | all-to-all | bytes 131072 | tf_op jit(solution)/shard_map/all_to_all | solution.py:167
  36.0 0.0 copy-start.1
  36.0 0.0 copy-start.2
  36.0 0.0 copy-start.3
  36.1 0.0 copy-start.4
  36.1 15.5 %all_to_all.27.bias = bf16[8,64,512]{2,1,0:T(8,128)(2,1)S(1)} all-to-all(bf16[8,64,512]{2,1,0:T(8,128)(2,1)S(1)} %broadcast_in_dim.31), channel_id=1, replica_groups=mesh['y'=4,'z'=16,'xh'=2,'xl'=2,'core'=2] {'y','xh'}, dimensions={0} | all-to-all | bytes 1048576 | tf_op jit(solution)/shard_map/all_to_all | solution.py:167
  51.5 0.0 copy-done.1
  51.5 0.0 copy-done.2
  51.5 0.0 copy-done.3
  51.5 0.0 copy-done.4
  51.6 3.0 %bias_sum.1 = bf16[8,64,512]{2,1,0:T(8,128)(2,1)S(1)} custom-call(bf16[4,32,512]{2,1,0:T(8,128)(2,1)S(1)} %bitcast.14, bf16[4,32,512]{2,1,0:T(8,128)(2,1)S(1)} %bitcast.16, bf16[4,32,512]{2,1,0:T(8,128)(2,1)S(1)} %bitcast.18, bf16[4,32,512]{2,1,0:T(8,128)(2,1)S(1)} %bitcast.20, bf16[8,64,512]{2,1,0:T(8,128)(2,1)S(1)} %all_to_all.27.bias), custom_call_target="tpu_custom_call" | custom-call | tf_op jit(solution)/shard_map/bias_sum/pallas_call | solution.py:111
  54.5 11.5 %all_to_all.28 = bf16[8,64,512]{2,1,0:T(8,128)(2,1)S(1)} all-to-all(bf16[8,64,512]{2,1,0:T(8,128)(2,1)S(1)} %bias_sum.1), channel_id=1, replica_groups=mesh['y'=4,'z'=16,'xh'=2,'xl'=2,'core'=2] {'y','xh'}, dimensions={0} | all-to-all | bytes 1048576 | tf_op jit(solution)/shard_map/all_to_all | solution.py:167
  66.1 0.1 reduce_sum.31
  66.2 0.7 broadcast_in_dim.33
  66.8 0.0 copy-start.5
  66.8 4.3 %all-to-all-start.4 = ((bf16[32,4,512]{2,1,0:T(4,128)(2,1)}), bf16[32,4,512]{2,1,0:T(4,128)(2,1)S(1)}, u32[]{:S(2)}, u32[]{:S(2)}) async-start(bf16[32,4,512]{2,1,0:T(4,128)(2,1)} %bitcast.5), calls=%async_computation.4 | async-start | bytes 262144 | tf_op jit(solution)/shard_map/all_to_all | solution.py:167
  71.2 0.0 copy-done.5
  71.2 0.1 copy.21.weight
  71.3 9.8 %input_grads.1 = (bf16[4,32,512]{2,1,0:T(8,128)(2,1)}, bf16[4,32,512]{2,1,0:T(8,128)(2,1)}, bf16[4,32,512]{2,1,0:T(8,128)(2,1)}) custom-call(bf16[4,32,512]{2,1,0:T(8,128)(2,1)S(1)} %bitcast.15, bf16[4,32,512]{2,1,0:T(8,128)(2,1)S(1)} %bitcast.17, bf16[4,32,512]{2,1,0:T(8,128)(2,1)S(1)} %bitcast.19, bf16[4,32,512]{2,1,0:T(8,128)(2,1)S(1)} %bitcast.21, ...), custom_call_target="tpu_custom_call" | custom-call | flops 335544320 | bytes 1048576 | tf_op jit(solution)/shard_map/input_grads/pallas_call | solution.py:126
  81.1 3.9 %all-to-all-done.4 = bf16[32,4,512]{2,1,0:T(4,128)(2,1)S(1)} async-done(((bf16[32,4,512]{2,1,0:T(4,128)(2,1)}), bf16[32,4,512]{2,1,0:T(4,128)(2,1)S(1)}, u32[]{:S(2)}, u32[]{:S(2)}) %all-to-all-start.4) | async-done | bytes 131104 | tf_op jit(solution)/shard_map/all_to_all | solution.py:167
  85.0 0.1 convert_reduce_fusion
  85.0 7.1 %all-gather = f32[4,4,512]{2,1,0:T(4,128)S(1)} all-gather(f32[2,4,512]{2,1,0:T(4,128)S(1)} %convert_reduce_fusion), channel_id=2, replica_groups=mesh['y'=4,'z'=16,'xh'=2,'xl'=2,'core'=2] {'core'}, dimensions={0}, use_global_device_ids=true | all-gather | bytes 49152 | tf_op jit(solution)/shard_map/all_gather | solution.py:189
  92.1 0.9 pair_grad.1
  (6 shorter events, 0.1 us)
Async XLA Ops:
  0.6 0.9 copy-start
  36.0 15.5 %copy-start.1 = (bf16[1,4,32,512]{3,2,1,0:T(8,128)(2,1)S(1)}, bf16[1,4,32,512]{3,2,1,0:T(8,128)(2,1)}, u32[]{:S(2)}) copy-start(bf16[1,4,32,512]{3,2,1,0:T(8,128)(2,1)} %param.6) | copy-start | bytes 393220
  36.0 15.5 %copy-start.2 = (bf16[1,4,32,512]{3,2,1,0:T(8,128)(2,1)S(1)}, bf16[1,4,32,512]{3,2,1,0:T(8,128)(2,1)}, u32[]{:S(2)}) copy-start(bf16[1,4,32,512]{3,2,1,0:T(8,128)(2,1)} %param.7) | copy-start | bytes 393220
  36.0 15.5 %copy-start.3 = (bf16[1,4,32,512]{3,2,1,0:T(8,128)(2,1)S(1)}, bf16[1,4,32,512]{3,2,1,0:T(8,128)(2,1)}, u32[]{:S(2)}) copy-start(bf16[1,4,32,512]{3,2,1,0:T(8,128)(2,1)} %param.8) | copy-start | bytes 393220
  36.1 15.5 %copy-start.4 = (bf16[1,4,32,512]{3,2,1,0:T(8,128)(2,1)S(1)}, bf16[1,4,32,512]{3,2,1,0:T(8,128)(2,1)}, u32[]{:S(2)}) copy-start(bf16[1,4,32,512]{3,2,1,0:T(8,128)(2,1)} %param.9) | copy-start | bytes 393220
  66.8 4.3 %copy-start.5 = (bf16[32,4]{0,1:T(4,128)(2,1)S(1)}, bf16[32,4]{0,1:T(4,128)(2,1)}, u32[]{:S(2)}) copy-start(bf16[32,4]{0,1:T(4,128)(2,1)} %param.11) | copy-start | bytes 772
  66.8 18.1 %all-to-all-start.4 = ((bf16[32,4,512]{2,1,0:T(4,128)(2,1)}), bf16[32,4,512]{2,1,0:T(4,128)(2,1)S(1)}, u32[]{:S(2)}, u32[]{:S(2)}) async-start(bf16[32,4,512]{2,1,0:T(4,128)(2,1)} %bitcast.5), calls=%async_computation.4 | async-start | bytes 262144 | tf_op jit(solution)/shard_map/all_to_all | solution.py:167

commit v4 on v3

v4 whole, which is shorter than its diff:
```python
import math

import jax
import jax.numpy as jnp
from jax import lax
from jax.experimental import pallas as pl
from jax.experimental.pallas import tpu as pltpu
from jax.sharding import Mesh
from jax.sharding import PartitionSpec as P

DH = 32
BLK = ("y", "z", "xh")
HEAD = ("xl", "core")
PLANE = ("y", "xh")
PLANE_ORDER = (5, 4, 7, 6, 1, 0, 3, 2)


def middle_first(count):
    return [(i + count // 2) % count for i in range(count)]


def place(y, xh):
    return PLANE_ORDER.index(2 * y + xh)


LIMIT = 24 * 1024 * 1024
LOG2E = math.log2(math.e)
OUTER = (((0,), (0,)), ((), ()))


def first_half(shape):
    return lax.broadcasted_iota(jnp.int32, shape, 1) < shape[1] // 2


def interleave(low, high):
    half = first_half(low.shape)
    even = jnp.where(half, low, pltpu.roll(high, 4, 1))
    odd = jnp.where(half, pltpu.roll(low, 4, 1), high)
    return jnp.stack([even, odd], axis=1).reshape(-1, low.shape[-1])


def separate(rows):
    pairs = rows.reshape(-1, 2, 8, rows.shape[-1])
    even, odd = pairs[:, 0], pairs[:, 1]
    half = first_half(even.shape)
    low = jnp.where(half, even, pltpu.roll(odd, 4, 1))
    high = jnp.where(half, pltpu.roll(even, 4, 1), odd)
    return low.reshape(-1, rows.shape[-1]), high.reshape(-1, rows.shape[-1])


def turned(rows):
    half = rows.shape[0] // 2
    return jnp.concatenate([rows[half:], rows[:half]], axis=0)


def bias_tile(bias, tile):
    low, high = (
        (bias[place(tile, part)].astype(jnp.float32) * LOG2E).reshape(-1, 8, bias.shape[-1])
        for part in range(2)
    )
    return turned(interleave(low, high))


def softmax_parts(query, keyset, wide):
    scores = lax.dot_general(query, keyset, OUTER, preferred_element_type=jnp.float32)
    scores = scores * (LOG2E * DH ** (-0.5)) + wide
    weights = jnp.exp2(scores - jnp.max(scores, axis=-1, keepdims=True))
    return weights, 1.0 / jnp.sum(weights, axis=-1, keepdims=True)


def sum_kernel(query, keyset, values, cotangent, bias, total):
    own = 2 * bias.shape[1]
    for tile in range(bias.shape[0] // 2):
        columns = slice(tile * own, (tile + 1) * own)
        wide = bias_tile(bias, tile)
        summed = None
        for row in range(query.shape[0]):
            weights, inverse = softmax_parts(query[row, :, columns], keyset[row], wide)
            dprobs = lax.dot_general(
                cotangent[row, :, columns], values[row], OUTER, preferred_element_type=jnp.float32
            )
            delta = jnp.sum(weights * dprobs, axis=-1, keepdims=True) * inverse
            dscores = (weights * inverse) * (dprobs - delta)
            summed = dscores if summed is None else summed + dscores
        for part, half in enumerate(separate(turned(summed))):
            total[place(tile, part)] = half.astype(jnp.bfloat16)


def bias_sum(query, keyset, values, cotangent, bias):
    held = pl.BlockSpec(memory_space=pltpu.VMEM)
    return pl.pallas_call(
        sum_kernel,
        in_specs=[held] * 5,
        out_specs=held,
        out_shape=jax.ShapeDtypeStruct(bias.shape, jnp.bfloat16),
        compiler_params=pltpu.CompilerParams(vmem_limit_bytes=LIMIT),
        name="bias_sum",
    )(query, keyset, values, cotangent, bias)


def inputs_kernel(query, keyset, values, cotangent, bias, *refs):
    grad_q, grad_k, grad_v, probs_low, dscores_low = refs
    own = 2 * bias.shape[1]
    scale = DH ** (-0.5)
    for row in range(query.shape[0]):
        for tile in range(bias.shape[0] // 2):
            columns = slice(tile * own, (tile + 1) * own)
            wide = bias_tile(bias, tile)
            weights, inverse = softmax_parts(query[row, :, columns], keyset[row], wide)
            probs = weights * inverse
            low = probs.astype(jnp.bfloat16)
            dprobs = lax.dot_general(
                cotangent[row, :, columns], values[row], OUTER, preferred_element_type=jnp.float32
            )
            delta = jnp.sum(low.astype(jnp.float32) * dprobs, axis=-1, keepdims=True)
            probs_low[row, columns] = low
            dscores_low[row, columns] = (probs * (dprobs - delta)).astype(jnp.bfloat16)
    for row in range(query.shape[0]):
        dscores = dscores_low[row]
        turned = lax.dot_general(
            keyset[row], dscores, (((1,), (1,)), ((), ())), preferred_element_type=jnp.float32
        )
        grad_q[row] = (turned * scale).astype(jnp.bfloat16)
        product = jnp.dot(query[row], dscores, preferred_element_type=jnp.float32)
        grad_k[row] = (product * scale).astype(jnp.bfloat16)
        grad_v[row] = jnp.dot(
            cotangent[row], probs_low[row], preferred_element_type=jnp.float32
        ).astype(jnp.bfloat16)


def input_grads(query, keyset, values, cotangent, bias):
    rows, depth, width = query.shape
    held = pl.BlockSpec(memory_space=pltpu.VMEM)
    whole = pl.BlockSpec(query.shape, lambda i: (0, 0, 0))
    shape = jax.ShapeDtypeStruct(query.shape, jnp.bfloat16)
    return pl.pallas_call(
        inputs_kernel,
        grid=(1,),
        in_specs=[held] * 5,
        out_specs=[whole] * 3,
        out_shape=[shape] * 3,
        scratch_shapes=[pltpu.VMEM((rows, width, width), jnp.bfloat16)] * 2,
        compiler_params=pltpu.CompilerParams(vmem_limit_bytes=LIMIT),
        cost_estimate=pl.CostEstimate(
            flops=10 * rows * depth * width * width,
            bytes_accessed=1 << 20,
            transcendentals=rows * width * width,
        ),
        name="input_grads",
    )(query, keyset, values, cotangent, bias)


def pair_kernel(weight, every_head, grad_pair):
    for head in range(every_head.shape[0]):
        scale = weight[:, head : head + 1].astype(jnp.float32)[:, :, None]
        term = scale * every_head[head][None]
        if head == 0:
            grad_pair[...] = term
        else:
            grad_pair[...] += term


def pair_grad(weight, every_head):
    held = pl.BlockSpec(memory_space=pltpu.VMEM)
    return pl.pallas_call(
        pair_kernel,
        in_specs=[held, held],
        out_specs=held,
        out_shape=jax.ShapeDtypeStruct(weight.shape[:1] + every_head.shape[1:], jnp.float32),
        compiler_params=pltpu.CompilerParams(vmem_limit_bytes=LIMIT),
        name="pair_grad",
    )(weight, every_head)


def exchange(blocks, axes, order=None):
    groups = None if order is None else [list(order)]
    return lax.all_to_all(blocks, axes, 0, 0, axis_index_groups=groups, tiled=True)


def shards(query, keyset, values, cotangent, pair_norm, bias_weight):
    nz = lax.axis_size("z")
    rows, width = pair_norm.shape[1:]
    query, keyset, values, cotangent = query[0], keyset[0], values[0], cotangent[0]

    partial = jnp.einsum("ch,cjk->hjk", bias_weight, pair_norm, preferred_element_type=jnp.float32)
    own = jnp.sum(exchange(partial, HEAD), axis=0).astype(jnp.bfloat16)
    line = jnp.broadcast_to(own[None], (nz, rows, width))
    line = exchange(line, "z", middle_first(nz)).reshape(nz * rows, width)
    planes = lax.axis_size(PLANE)
    bias = exchange(jnp.broadcast_to(line[None], (planes,) + line.shape), PLANE, PLANE_ORDER)

    total = bias_sum(query, keyset, values, cotangent, bias)
    line = jnp.sum(exchange(total, PLANE, PLANE_ORDER).astype(jnp.float32), axis=0).astype(jnp.bfloat16)
    line = exchange(line.reshape(nz, rows, width), "z", middle_first(nz))
    grads = input_grads(query, keyset, values, cotangent, bias)
    line, *grads = lax.optimization_barrier((line, *grads))
    own = jnp.sum(line.astype(jnp.float32), axis=0)
    every_head = lax.all_gather(own, HEAD, axis=0)
    grad_pair = pair_grad(bias_weight, every_head)
    return grads[0][None], grads[1][None], grads[2][None], grad_pair


def solution(mesh):
    fine = Mesh(mesh.devices.reshape(4, 16, 2, 2, 2), BLK + HEAD)
    four = P(HEAD, BLK, None, None)
    three = P(HEAD, BLK, None)
    return jax.shard_map(
        shards,
        mesh=fine,
        in_specs=(four, four, four, four, three, P(HEAD, None)),
        out_specs=(four, four, four, three),
        check_vma=False,
    )
```

time: 93.4 us -> 86.1 us (0.922)
  starting transfers between devices: 4.32 us -> 11.6 us
  Pallas kernels: 13.7 us -> 8.34 us
  blocking collectives: 67.6 us -> 62.3 us
  waiting for transfers between devices: 3.9 us -> 0.01 us
    all_to_all x1, starting transfers between devices: 4.32 us -> 11.6 us  [exchange(): lax.all_to_all(blocks, axes, 0, 0, axis_index_groups=groups, tiled=True)]
    all_to_all x4, blocking collectives: 60.5 us -> 53.5 us  [exchange(): lax.all_to_all(blocks, axes, 0, 0, axis_index_groups=groups, tiled=True)]
    pallas_call x2, Pallas kernels: 12.8 us -> 7.43 us  [the longest x1 4.38 us: input_grads(): pl.pallas_call(inputs_kernel, grid=(1,), in_specs=[held] * 5, out_specs=[...]
    all_to_all x1, waiting for transfers between devices: 3.9 us -> 0.01 us  [exchange(): lax.all_to_all(blocks, axes, 0, 0, axis_index_groups=groups, tiled=True)]
    all_gather x1, blocking collectives: 7.11 us -> 8.74 us  [shards(): every_head = lax.all_gather(own, HEAD, axis=0)]
  transfers between devices with their start and end apart: 1 -> 1, of which waited for: 1 -> 0; matrix products, arithmetic and copies ran while one was open for 0% -> 0% of each run, Pallas kernels for 11% -> 5%
where the time goes in v4:
time: 86.1 us; the launch traced here: 85.7 us
  blocking collectives  62.3 us (72%)
  starting transfers between devices  11.6 us (13%)
  Pallas kernels  8.34 us (10%)
  local copies, waits for them, and re-layouts  1.78 us (2%)
    all_to_all x4, blocking collectives, exchange(): lax.all_to_all(blocks, axes, 0, 0, axis_index_groups=groups, tiled=True)  53.5 us
    all_to_all x1, starting transfers between devices, exchange(): lax.all_to_all(blocks, axes, 0, 0, axis_index_groups=groups, tiled=True)  11.6 us
    all_gather x1, blocking collectives, shards(): every_head = lax.all_gather(own, HEAD, axis=0)  8.74 us
    pallas_call x1, Pallas kernels, input_grads(): pl.pallas_call(inputs_kernel, grid=(1,), in_specs=[held] * 5, out_specs=[...  4.38 us
    pallas_call x1, Pallas kernels, bias_sum(): pl.pallas_call(sum_kernel, in_specs=[held] * 5, out_specs=held, out_shape...  3.05 us
  transfers between devices with their start and end apart: 1, of which 0 were waited for; matrix products, arithmetic and copies ran while one was open for 0% of the time, Pallas kernels for 5%

profile of v4, /device:TPU:1, one launch (start us, length us, event | category | flops | bytes accessed | tf_op | source)
XLA Modules:
  0.0 85.7 jit_solution(3694953635679197465)
XLA Ops:
  0.6 0.0 copy-start
  0.6 0.9 %copy-done = bf16[32,4,512]{2,1,0:T(4,128)(2,1)S(1)} copy-done((bf16[32,4,512]{2,1,0:T(4,128)(2,1)S(1)}, bf16[32,4,512]{2,1,0:T(4,128)(2,1)}, u32[]{:S(2)}) %copy-start) | copy-done | bytes 131096
  1.5 0.8 fusion
  2.4 12.4 %all_to_all.25 = f32[4,4,512]{2,1,0:T(4,128)S(1)} all-to-all(f32[4,4,512]{2,1,0:T(4,128)S(1)} %copy.19), channel_id=1, replica_groups=mesh['y'=4,'z'=16,'xh'=2,'xl'=2,'core'=2] {'xl','core'}, dimensions={0} | all-to-all | bytes 65536 | tf_op jit(solution)/shard_map/all_to_all | solution.py:177
  14.8 16.1 %all_to_all.26 = bf16[16,4,512]{2,1,0:T(4,128)(2,1)S(1)} all-to-all(bf16[16,4,512]{2,1,0:T(4,128)(2,1)S(1)} %broadcast_in_dim.22), channel_id=1, replica_groups={{64,72,80,88,96,104,112,120,0,8,16,24,32,40,48,56},{65,73,81,89,97,105,..., dimensions={0} | all-to-all | bytes 131072 | tf_op jit(solution)/shard_map/all_to_all | solution.py:177
  31.0 0.0 copy-start.1
  31.0 0.0 copy-start.2
  31.0 0.0 copy-start.3
  31.0 0.0 copy-start.4
  31.0 13.2 %all_to_all.27.bias = bf16[8,64,512]{2,1,0:T(8,128)(2,1)S(1)} all-to-all(bf16[8,64,512]{2,1,0:T(8,128)(2,1)S(1)} %broadcast_in_dim.24), channel_id=1, replica_groups={{260,256,388,384,4,0,132,128},{261,257,389,385,5,1,133,129},{262,258,39..., dimensions={0} | all-to-all | bytes 1048576 | tf_op jit(solution)/shard_map/all_to_all | solution.py:177
  44.3 0.0 copy-done.1
  44.3 0.0 copy-done.2
  44.3 0.0 copy-done.3
  44.3 0.0 copy-done.4
  44.3 3.0 %bias_sum.1 = bf16[8,64,512]{2,1,0:T(8,128)(2,1)S(1)} custom-call(bf16[4,32,512]{2,1,0:T(8,128)(2,1)S(1)} %bitcast.11, bf16[4,32,512]{2,1,0:T(8,128)(2,1)S(1)} %bitcast.13, bf16[4,32,512]{2,1,0:T(8,128)(2,1)S(1)} %bitcast.15, bf16[4,32,512]{2,1,0:T(8,128)(2,1)S(1)} %bitcast.17, bf16[8,64,512]{2,1,0:T(8,128)(2,1)S(1)} %all_to_all.27.bias), custom_call_target="tpu_custom_call" | custom-call | tf_op jit(solution)/shard_map/bias_sum/pallas_call | solution.py:91
  47.3 11.8 %all_to_all.28 = bf16[8,64,512]{2,1,0:T(8,128)(2,1)S(1)} all-to-all(bf16[8,64,512]{2,1,0:T(8,128)(2,1)S(1)} %bias_sum.1), channel_id=1, replica_groups={{260,256,388,384,4,0,132,128},{261,257,389,385,5,1,133,129},{262,258,39..., dimensions={0} | all-to-all | bytes 1048576 | tf_op jit(solution)/shard_map/all_to_all | solution.py:177
  59.1 0.1 reduce_sum.31
  59.2 0.7 reshape.15
  59.9 0.0 copy-start.5
  59.9 11.6 %all-to-all-start.4 = ((bf16[16,4,512]{2,1,0:T(4,128)(2,1)}), bf16[16,4,512]{2,1,0:T(4,128)(2,1)S(1)}, u32[]{:S(2)}, u32[]{:S(2)}) async-start(bf16[16,4,512]{2,1,0:T(4,128)(2,1)} %reshape.15), calls=%async_computation.4 | async-start | bytes 131072 | tf_op jit(solution)/shard_map/all_to_all | solution.py:177
  71.5 0.0 copy-done.5
  71.5 0.1 copy.21.weight
  71.6 4.4 %input_grads.1 = (bf16[4,32,512]{2,1,0:T(8,128)(2,1)}, bf16[4,32,512]{2,1,0:T(8,128)(2,1)}, bf16[4,32,512]{2,1,0:T(8,128)(2,1)}) custom-call(bf16[4,32,512]{2,1,0:T(8,128)(2,1)S(1)} %bitcast.12, bf16[4,32,512]{2,1,0:T(8,128)(2,1)S(1)} %bitcast.14, bf16[4,32,512]{2,1,0:T(8,128)(2,1)S(1)} %bitcast.16, bf16[4,32,512]{2,1,0:T(8,128)(2,1)S(1)} %bitcast.18, ...), custom_call_target="tpu_custom_call" | custom-call | flops 335544320 | bytes 1048576 | tf_op jit(solution)/shard_map/input_grads/pallas_call | solution.py:136
  76.0 0.0 all-to-all-done.4
  76.1 8.7 %all-gather.1.every_head = f32[4,4,512]{2,1,0:T(4,128)S(1)} all-gather(f32[1,4,512]{2,1,0:T(4,128)S(1)} %bitcast.19), channel_id=2, replica_groups=mesh['y'=4,'z'=16,'xh'=2,'xl'=2,'core'=2] {'xl','core'}, dimensions={0}, use_global_device_ids=true | all-gather | bytes 40960 | tf_op jit(solution)/shard_map/all_gather | solution.py:198
  84.8 0.9 %pair_grad.1 = f32[32,4,512]{2,1,0:T(4,128)} custom-call(bf16[32,4]{1,0:T(8,128)(2,1)S(1)} %copy.21.weight, f32[4,4,512]{2,1,0:T(4,128)S(1)} %all-gather.1.every_head), custom_call_target="tpu_custom_call" | custom-call | tf_op jit(solution)/shard_map/pair_grad/pallas_call | solution.py:165
  (6 shorter events, 0.2 us)
Async XLA Ops:
  0.6 0.9 %copy-start = (bf16[32,4,512]{2,1,0:T(4,128)(2,1)S(1)}, bf16[32,4,512]{2,1,0:T(4,128)(2,1)}, u32[]{:S(2)}) copy-start(bf16[32,4,512]{2,1,0:T(4,128)(2,1)} %param.10) | copy-start | bytes 393220
  31.0 13.3 %copy-start.1 = (bf16[1,4,32,512]{3,2,1,0:T(8,128)(2,1)S(1)}, bf16[1,4,32,512]{3,2,1,0:T(8,128)(2,1)}, u32[]{:S(2)}) copy-start(bf16[1,4,32,512]{3,2,1,0:T(8,128)(2,1)} %param.6) | copy-start | bytes 393220
  31.0 13.3 %copy-start.2 = (bf16[1,4,32,512]{3,2,1,0:T(8,128)(2,1)S(1)}, bf16[1,4,32,512]{3,2,1,0:T(8,128)(2,1)}, u32[]{:S(2)}) copy-start(bf16[1,4,32,512]{3,2,1,0:T(8,128)(2,1)} %param.7) | copy-start | bytes 393220
  31.0 13.3 %copy-start.3 = (bf16[1,4,32,512]{3,2,1,0:T(8,128)(2,1)S(1)}, bf16[1,4,32,512]{3,2,1,0:T(8,128)(2,1)}, u32[]{:S(2)}) copy-start(bf16[1,4,32,512]{3,2,1,0:T(8,128)(2,1)} %param.8) | copy-start | bytes 393220
  31.0 13.2 %copy-start.4 = (bf16[1,4,32,512]{3,2,1,0:T(8,128)(2,1)S(1)}, bf16[1,4,32,512]{3,2,1,0:T(8,128)(2,1)}, u32[]{:S(2)}) copy-start(bf16[1,4,32,512]{3,2,1,0:T(8,128)(2,1)} %param.9) | copy-start | bytes 393220
  59.9 11.7 %copy-start.5 = (bf16[32,4]{0,1:T(4,128)(2,1)S(1)}, bf16[32,4]{0,1:T(4,128)(2,1)}, u32[]{:S(2)}) copy-start(bf16[32,4]{0,1:T(4,128)(2,1)} %param.11) | copy-start | bytes 772
  59.9 16.1 %all-to-all-start.4 = ((bf16[16,4,512]{2,1,0:T(4,128)(2,1)}), bf16[16,4,512]{2,1,0:T(4,128)(2,1)S(1)}, u32[]{:S(2)}, u32[]{:S(2)}) async-start(bf16[16,4,512]{2,1,0:T(4,128)(2,1)} %reshape.15), calls=%async_computation.4 | async-start | bytes 131072 | tf_op jit(solution)/shard_map/all_to_all | solution.py:177

commit v5 on v4

--- a/solution.py
+++ b/solution.py
@@ -151,9 +151,9 @@
 
 
 def pair_kernel(weight, every_head, grad_pair):
-    for head in range(every_head.shape[0]):
+    for head in range(4):
         scale = weight[:, head : head + 1].astype(jnp.float32)[:, :, None]
-        term = scale * every_head[head][None]
+        term = scale * every_head[head % 2, 1 - head // 2][None]
         if head == 0:
             grad_pair[...] = term
         else:
@@ -166,7 +166,7 @@
         pair_kernel,
         in_specs=[held, held],
         out_specs=held,
-        out_shape=jax.ShapeDtypeStruct(weight.shape[:1] + every_head.shape[1:], jnp.float32),
+        out_shape=jax.ShapeDtypeStruct(weight.shape[:1] + every_head.shape[2:], jnp.float32),
         compiler_params=pltpu.CompilerParams(vmem_limit_bytes=LIMIT),
         name="pair_grad",
     )(weight, every_head)
@@ -191,11 +191,13 @@
 
     total = bias_sum(query, keyset, values, cotangent, bias)
     line = jnp.sum(exchange(total, PLANE, PLANE_ORDER).astype(jnp.float32), axis=0).astype(jnp.bfloat16)
-    line = exchange(line.reshape(nz, rows, width), "z", middle_first(nz))
+    line = jnp.broadcast_to(line.reshape(nz, 1, rows, width), (nz, 2, rows, width))
+    order = [2 * z + xl for z in middle_first(nz) for xl in (1, 0)]
+    line = exchange(line.reshape(nz * 2, rows, width), ("z", "xl"), order)
     grads = input_grads(query, keyset, values, cotangent, bias)
     line, *grads = lax.optimization_barrier((line, *grads))
-    own = jnp.sum(line.astype(jnp.float32), axis=0)
-    every_head = lax.all_gather(own, HEAD, axis=0)
+    own = jnp.sum(line.astype(jnp.float32).reshape(nz, 2, rows, width), axis=0)
+    every_head = lax.all_gather(own, "core", axis=0)
     grad_pair = pair_grad(bias_weight, every_head)
     return grads[0][None], grads[1][None], grads[2][None], grad_pair
 

time: 86.1 us -> 84.2 us (0.978)
  blocking collectives: 62.3 us -> 59.2 us
  starting transfers between devices: 11.6 us -> 12.7 us
    all_gather x1, blocking collectives: 8.74 us -> 5.71 us  [shards(): every_head = lax.all_gather(own, 'core', axis=0)]
    all_to_all x1, starting transfers between devices: 11.6 us -> 12.7 us  [exchange(): lax.all_to_all(blocks, axes, 0, 0, axis_index_groups=groups, tiled=True)]
where the time goes in v5:
time: 84.2 us; the launch traced here: 83.8 us
  blocking collectives  59.2 us (70%)
  starting transfers between devices  12.7 us (15%)
  Pallas kernels  8.33 us (10%)
  local copies, waits for them, and re-layouts  1.85 us (2%)
    all_to_all x4, blocking collectives, exchange(): lax.all_to_all(blocks, axes, 0, 0, axis_index_groups=groups, tiled=True)  53.5 us
    all_to_all x1, starting transfers between devices, exchange(): lax.all_to_all(blocks, axes, 0, 0, axis_index_groups=groups, tiled=True)  12.7 us
    all_gather x1, blocking collectives, shards(): every_head = lax.all_gather(own, 'core', axis=0)  5.71 us
    pallas_call x1, Pallas kernels, input_grads(): pl.pallas_call(inputs_kernel, grid=(1,), in_specs=[held] * 5, out_specs=[...  4.37 us
    pallas_call x1, Pallas kernels, bias_sum(): pl.pallas_call(sum_kernel, in_specs=[held] * 5, out_specs=held, out_shape...  3.05 us
  transfers between devices with their start and end apart: 1, of which 0 were waited for; matrix products, arithmetic and copies ran while one was open for 0% of the time, Pallas kernels for 5%

profile of v5, /device:TPU:1, one launch (start us, length us, event | category | flops | bytes accessed | tf_op | source)
XLA Modules:
  0.0 83.8 jit_solution(4899433788868175586)
XLA Ops:
  0.6 0.0 copy-start
  0.6 0.9 %copy-done = bf16[32,4,512]{2,1,0:T(4,128)(2,1)S(1)} copy-done((bf16[32,4,512]{2,1,0:T(4,128)(2,1)S(1)}, bf16[32,4,512]{2,1,0:T(4,128)(2,1)}, u32[]{:S(2)}) %copy-start) | copy-done | bytes 131096
  1.5 0.8 fusion
  2.4 12.4 %all_to_all.25 = f32[4,4,512]{2,1,0:T(4,128)S(1)} all-to-all(f32[4,4,512]{2,1,0:T(4,128)S(1)} %copy.19), channel_id=1, replica_groups=mesh['y'=4,'z'=16,'xh'=2,'xl'=2,'core'=2] {'xl','core'}, dimensions={0} | all-to-all | bytes 65536 | tf_op jit(solution)/shard_map/all_to_all | solution.py:177
  14.8 16.1 %all_to_all.26 = bf16[16,4,512]{2,1,0:T(4,128)(2,1)S(1)} all-to-all(bf16[16,4,512]{2,1,0:T(4,128)(2,1)S(1)} %broadcast_in_dim.29), channel_id=1, replica_groups={{64,72,80,88,96,104,112,120,0,8,16,24,32,40,48,56},{65,73,81,89,97,105,..., dimensions={0} | all-to-all | bytes 131072 | tf_op jit(solution)/shard_map/all_to_all | solution.py:177
  31.0 0.0 copy-start.1
  31.0 0.0 copy-start.2
  31.0 0.0 copy-start.3
  31.0 0.0 copy-start.4
  31.0 13.2 %all_to_all.27.bias = bf16[8,64,512]{2,1,0:T(8,128)(2,1)S(1)} all-to-all(bf16[8,64,512]{2,1,0:T(8,128)(2,1)S(1)} %broadcast_in_dim.31), channel_id=1, replica_groups={{260,256,388,384,4,0,132,128},{261,257,389,385,5,1,133,129},{262,258,39..., dimensions={0} | all-to-all | bytes 1048576 | tf_op jit(solution)/shard_map/all_to_all | solution.py:177
  44.3 0.0 copy-done.1
  44.3 0.0 copy-done.2
  44.3 0.0 copy-done.3
  44.3 0.0 copy-done.4
  44.3 3.0 %bias_sum.1 = bf16[8,64,512]{2,1,0:T(8,128)(2,1)S(1)} custom-call(bf16[4,32,512]{2,1,0:T(8,128)(2,1)S(1)} %bitcast.14, bf16[4,32,512]{2,1,0:T(8,128)(2,1)S(1)} %bitcast.16, bf16[4,32,512]{2,1,0:T(8,128)(2,1)S(1)} %bitcast.18, bf16[4,32,512]{2,1,0:T(8,128)(2,1)S(1)} %bitcast.20, bf16[8,64,512]{2,1,0:T(8,128)(2,1)S(1)} %all_to_all.27.bias), custom_call_target="tpu_custom_call" | custom-call | tf_op jit(solution)/shard_map/bias_sum/pallas_call | solution.py:91
  47.3 11.8 %all_to_all.28 = bf16[8,64,512]{2,1,0:T(8,128)(2,1)S(1)} all-to-all(bf16[8,64,512]{2,1,0:T(8,128)(2,1)S(1)} %bias_sum.1), channel_id=1, replica_groups={{260,256,388,384,4,0,132,128},{261,257,389,385,5,1,133,129},{262,258,39..., dimensions={0} | all-to-all | bytes 1048576 | tf_op jit(solution)/shard_map/all_to_all | solution.py:177
  59.1 0.1 reduce_sum.31
  59.2 0.7 broadcast_in_dim.33
  59.9 0.0 copy-start.5
  59.9 12.7 %all-to-all-start.4 = ((bf16[32,4,512]{2,1,0:T(4,128)(2,1)}), bf16[32,4,512]{2,1,0:T(4,128)(2,1)S(1)}, u32[]{:S(2)}, u32[]{:S(2)}) async-start(bf16[32,4,512]{2,1,0:T(4,128)(2,1)} %bitcast.5), calls=%async_computation.4 | async-start | bytes 262144 | tf_op jit(solution)/shard_map/all_to_all | solution.py:177
  72.6 0.0 copy-done.5
  72.7 0.1 copy.21.weight
  72.8 4.4 %input_grads.1 = (bf16[4,32,512]{2,1,0:T(8,128)(2,1)}, bf16[4,32,512]{2,1,0:T(8,128)(2,1)}, bf16[4,32,512]{2,1,0:T(8,128)(2,1)}) custom-call(bf16[4,32,512]{2,1,0:T(8,128)(2,1)S(1)} %bitcast.15, bf16[4,32,512]{2,1,0:T(8,128)(2,1)S(1)} %bitcast.17, bf16[4,32,512]{2,1,0:T(8,128)(2,1)S(1)} %bitcast.19, bf16[4,32,512]{2,1,0:T(8,128)(2,1)S(1)} %bitcast.21, ...), custom_call_target="tpu_custom_call" | custom-call | flops 335544320 | bytes 1048576 | tf_op jit(solution)/shard_map/input_grads/pallas_call | solution.py:136
  77.1 0.0 all-to-all-done.4
  77.1 0.1 convert_reduce_fusion
  77.2 5.7 %all-gather = f32[4,4,512]{2,1,0:T(4,128)S(1)} all-gather(f32[2,4,512]{2,1,0:T(4,128)S(1)} %convert_reduce_fusion), channel_id=2, replica_groups=mesh['y'=4,'z'=16,'xh'=2,'xl'=2,'core'=2] {'core'}, dimensions={0}, use_global_device_ids=true | all-gather | bytes 49152 | tf_op jit(solution)/shard_map/all_gather | solution.py:200
  82.9 0.9 %pair_grad.1 = f32[32,4,512]{2,1,0:T(4,128)} custom-call(bf16[32,4]{1,0:T(8,128)(2,1)S(1)} %copy.21.weight, f32[2,2,4,512]{3,2,1,0:T(4,128)S(1)} %bitcast.22), custom_call_target="tpu_custom_call" | custom-call | tf_op jit(solution)/shard_map/pair_grad/pallas_call | solution.py:165
  (6 shorter events, 0.1 us)
Async XLA Ops:
  0.6 0.9 %copy-start = (bf16[32,4,512]{2,1,0:T(4,128)(2,1)S(1)}, bf16[32,4,512]{2,1,0:T(4,128)(2,1)}, u32[]{:S(2)}) copy-start(bf16[32,4,512]{2,1,0:T(4,128)(2,1)} %param.10) | copy-start | bytes 393220
  31.0 13.3 %copy-start.1 = (bf16[1,4,32,512]{3,2,1,0:T(8,128)(2,1)S(1)}, bf16[1,4,32,512]{3,2,1,0:T(8,128)(2,1)}, u32[]{:S(2)}) copy-start(bf16[1,4,32,512]{3,2,1,0:T(8,128)(2,1)} %param.6) | copy-start | bytes 393220
  31.0 13.3 %copy-start.2 = (bf16[1,4,32,512]{3,2,1,0:T(8,128)(2,1)S(1)}, bf16[1,4,32,512]{3,2,1,0:T(8,128)(2,1)}, u32[]{:S(2)}) copy-start(bf16[1,4,32,512]{3,2,1,0:T(8,128)(2,1)} %param.7) | copy-start | bytes 393220
  31.0 13.3 %copy-start.3 = (bf16[1,4,32,512]{3,2,1,0:T(8,128)(2,1)S(1)}, bf16[1,4,32,512]{3,2,1,0:T(8,128)(2,1)}, u32[]{:S(2)}) copy-start(bf16[1,4,32,512]{3,2,1,0:T(8,128)(2,1)} %param.8) | copy-start | bytes 393220
  31.0 13.2 %copy-start.4 = (bf16[1,4,32,512]{3,2,1,0:T(8,128)(2,1)S(1)}, bf16[1,4,32,512]{3,2,1,0:T(8,128)(2,1)}, u32[]{:S(2)}) copy-start(bf16[1,4,32,512]{3,2,1,0:T(8,128)(2,1)} %param.9) | copy-start | bytes 393220
  59.9 12.7 %copy-start.5 = (bf16[32,4]{0,1:T(4,128)(2,1)S(1)}, bf16[32,4]{0,1:T(4,128)(2,1)}, u32[]{:S(2)}) copy-start(bf16[32,4]{0,1:T(4,128)(2,1)} %param.11) | copy-start | bytes 772
  59.9 17.2 %all-to-all-start.4 = ((bf16[32,4,512]{2,1,0:T(4,128)(2,1)}), bf16[32,4,512]{2,1,0:T(4,128)(2,1)S(1)}, u32[]{:S(2)}, u32[]{:S(2)}) async-start(bf16[32,4,512]{2,1,0:T(4,128)(2,1)} %bitcast.5), calls=%async_computation.4 | async-start | bytes 262144 | tf_op jit(solution)/shard_map/all_to_all | solution.py:177

commit v6 on v5

--- a/solution.py
+++ b/solution.py
@@ -70,9 +70,10 @@
 
 def sum_kernel(query, keyset, values, cotangent, bias, total):
     own = 2 * bias.shape[1]
-    for tile in range(bias.shape[0] // 2):
-        columns = slice(tile * own, (tile + 1) * own)
-        wide = bias_tile(bias, tile)
+    for pair in range(bias.shape[0] // 4):
+        tiles = (2 * pair, 2 * pair + 1)
+        columns = slice(tiles[0] * own, (tiles[1] + 1) * own)
+        wide = jnp.concatenate([bias_tile(bias, tile) for tile in tiles], axis=0)
         summed = None
         for row in range(query.shape[0]):
             weights, inverse = softmax_parts(query[row, :, columns], keyset[row], wide)
@@ -82,8 +83,10 @@
             delta = jnp.sum(weights * dprobs, axis=-1, keepdims=True) * inverse
             dscores = (weights * inverse) * (dprobs - delta)
             summed = dscores if summed is None else summed + dscores
-        for part, half in enumerate(separate(turned(summed))):
-            total[place(tile, part)] = half.astype(jnp.bfloat16)
+        for index, tile in enumerate(tiles):
+            rows = summed[index * own : (index + 1) * own]
+            for part, half in enumerate(separate(turned(rows))):
+                total[place(tile, part)] = half.astype(jnp.bfloat16)
 
 
 def bias_sum(query, keyset, values, cotangent, bias):
@@ -150,6 +153,49 @@
     )(query, keyset, values, cotangent, bias)
 
 
+def fold_kernel(parts, line):
+    summed = parts[0].astype(jnp.float32)
+    for part in range(1, parts.shape[0]):
+        summed = summed + parts[part].astype(jnp.float32)
+    rows = line.shape[2]
+    for block in range(line.shape[0]):
+        low = summed[block * rows : (block + 1) * rows].astype(jnp.bfloat16)
+        for copy in range(line.shape[1]):
+            line[block, copy] = low
+
+
+def fold(parts, rows, copies):
+    held = pl.BlockSpec(memory_space=pltpu.VMEM)
+    shape = (parts.shape[1] // rows, copies, rows, parts.shape[2])
+    return pl.pallas_call(
+        fold_kernel,
+        in_specs=[held],
+        out_specs=held,
+        out_shape=jax.ShapeDtypeStruct(shape, jnp.bfloat16),
+        compiler_params=pltpu.CompilerParams(vmem_limit_bytes=LIMIT),
+        name="fold",
+    )(parts)
+
+
+def project_kernel(weight, pair_norm, partial):
+    scales = weight[...].astype(jnp.float32)
+    wide = pair_norm[...].astype(jnp.float32)
+    for head in range(partial.shape[0]):
+        partial[head] = jnp.sum(scales[:, head : head + 1][:, :, None] * wide, axis=0)
+
+
+def project(weight, pair_norm):
+    held = pl.BlockSpec(memory_space=pltpu.VMEM)
+    return pl.pallas_call(
+        project_kernel,
+        in_specs=[held, held],
+        out_specs=held,
+        out_shape=jax.ShapeDtypeStruct(weight.shape[1:] + pair_norm.shape[1:], jnp.float32),
+        compiler_params=pltpu.CompilerParams(vmem_limit_bytes=LIMIT),
+        name="project",
+    )(weight, pair_norm)
+
+
 def pair_kernel(weight, every_head, grad_pair):
     for head in range(4):
         scale = weight[:, head : head + 1].astype(jnp.float32)[:, :, None]
@@ -190,8 +236,7 @@
     bias = exchange(jnp.broadcast_to(line[None], (planes,) + line.shape), PLANE, PLANE_ORDER)
 
     total = bias_sum(query, keyset, values, cotangent, bias)
-    line = jnp.sum(exchange(total, PLANE, PLANE_ORDER).astype(jnp.float32), axis=0).astype(jnp.bfloat16)
-    line = jnp.broadcast_to(line.reshape(nz, 1, rows, width), (nz, 2, rows, width))
+    line = fold(exchange(total, PLANE, PLANE_ORDER), rows, 2)
     order = [2 * z + xl for z in middle_first(nz) for xl in (1, 0)]
     line = exchange(line.reshape(nz * 2, rows, width), ("z", "xl"), order)
     grads = input_grads(query, keyset, values, cotangent, bias)

time: 84.2 us -> 83.6 us (level)
  no operation moved by 1% of the time
where the time goes in v6:
time: 83.6 us; the launch traced here: 83.3 us
  blocking collectives  59.2 us (71%)
  starting transfers between devices  12.7 us (15%)
  Pallas kernels  8.6 us (10%)
  local copies, waits for them, and re-layouts  1.13 us (1%)
    all_to_all x4, blocking collectives, exchange(): lax.all_to_all(blocks, axes, 0, 0, axis_index_groups=groups, tiled=True)  53.5 us
    all_to_all x1, starting transfers between devices, exchange(): lax.all_to_all(blocks, axes, 0, 0, axis_index_groups=groups, tiled=True)  12.7 us
    all_gather x1, blocking collectives, shards(): every_head = lax.all_gather(own, 'core', axis=0)  5.73 us
    pallas_call x1, Pallas kernels, input_grads(): pl.pallas_call(inputs_kernel, grid=(1,), in_specs=[held] * 5, out_specs=[...  4.37 us
    pallas_call x1, Pallas kernels, bias_sum(): pl.pallas_call(sum_kernel, in_specs=[held] * 5, out_specs=held, out_shape...  2.58 us
  transfers between devices with their start and end apart: 1, of which 0 were waited for; matrix products, arithmetic and copies ran while one was open for 0% of the time, Pallas kernels for 5%

profile of v6, /device:TPU:1, one launch (start us, length us, event | category | flops | bytes accessed | tf_op | source)
XLA Modules:
  0.0 83.3 jit_solution(9574618438444368896)
XLA Ops:
  0.6 0.0 copy-start
  0.6 0.9 %copy-done = bf16[32,4,512]{2,1,0:T(4,128)(2,1)S(1)} copy-done((bf16[32,4,512]{2,1,0:T(4,128)(2,1)S(1)}, bf16[32,4,512]{2,1,0:T(4,128)(2,1)}, u32[]{:S(2)}) %copy-start) | copy-done | bytes 131096
  1.5 0.8 fusion
  2.4 12.4 %all_to_all.25 = f32[4,4,512]{2,1,0:T(4,128)S(1)} all-to-all(f32[4,4,512]{2,1,0:T(4,128)S(1)} %copy.13), channel_id=1, replica_groups=mesh['y'=4,'z'=16,'xh'=2,'xl'=2,'core'=2] {'xl','core'}, dimensions={0} | all-to-all | bytes 65536 | tf_op jit(solution)/shard_map/all_to_all | solution.py:223
  14.8 16.1 %all_to_all.26 = bf16[16,4,512]{2,1,0:T(4,128)(2,1)S(1)} all-to-all(bf16[16,4,512]{2,1,0:T(4,128)(2,1)S(1)} %broadcast_in_dim.22), channel_id=1, replica_groups={{64,72,80,88,96,104,112,120,0,8,16,24,32,40,48,56},{65,73,81,89,97,105,..., dimensions={0} | all-to-all | bytes 131072 | tf_op jit(solution)/shard_map/all_to_all | solution.py:223
  31.0 0.0 copy-start.1
  31.0 0.0 copy-start.2
  31.0 0.0 copy-start.3
  31.0 0.0 copy-start.4
  31.0 13.2 %all_to_all.27.bias = bf16[8,64,512]{2,1,0:T(8,128)(2,1)S(1)} all-to-all(bf16[8,64,512]{2,1,0:T(8,128)(2,1)S(1)} %broadcast_in_dim.24), channel_id=1, replica_groups={{260,256,388,384,4,0,132,128},{261,257,389,385,5,1,133,129},{262,258,39..., dimensions={0} | all-to-all | bytes 1048576 | tf_op jit(solution)/shard_map/all_to_all | solution.py:223
  44.3 0.0 copy-done.1
  44.3 0.0 copy-done.2
  44.3 0.0 copy-done.3
  44.3 0.0 copy-done.4
  44.3 2.6 %bias_sum.1 = bf16[8,64,512]{2,1,0:T(8,128)(2,1)S(1)} custom-call(bf16[4,32,512]{2,1,0:T(8,128)(2,1)S(1)} %bitcast.14, bf16[4,32,512]{2,1,0:T(8,128)(2,1)S(1)} %bitcast.16, bf16[4,32,512]{2,1,0:T(8,128)(2,1)S(1)} %bitcast.18, bf16[4,32,512]{2,1,0:T(8,128)(2,1)S(1)} %bitcast.20, bf16[8,64,512]{2,1,0:T(8,128)(2,1)S(1)} %all_to_all.27.bias), custom_call_target="tpu_custom_call" | custom-call | tf_op jit(solution)/shard_map/bias_sum/pallas_call | solution.py:94
  46.9 11.8 %all_to_all.28.parts = bf16[8,64,512]{2,1,0:T(8,128)(2,1)S(1)} all-to-all(bf16[8,64,512]{2,1,0:T(8,128)(2,1)S(1)} %bias_sum.1), channel_id=1, replica_groups={{260,256,388,384,4,0,132,128},{261,257,389,385,5,1,133,129},{262,258,39..., dimensions={0} | all-to-all | bytes 1048576 | tf_op jit(solution)/shard_map/all_to_all | solution.py:223
  58.7 0.7 fold.1
  59.4 0.0 copy-start.5
  59.4 12.7 %all-to-all-start.4 = ((bf16[32,4,512]{2,1,0:T(4,128)(2,1)}), bf16[32,4,512]{2,1,0:T(4,128)(2,1)S(1)}, u32[]{:S(2)}, u32[]{:S(2)}) async-start(bf16[32,4,512]{2,1,0:T(4,128)(2,1)} %bitcast.5), calls=%async_computation.4 | async-start | bytes 262144 | tf_op jit(solution)/shard_map/all_to_all | solution.py:223
  72.1 0.0 copy-done.5
  72.1 0.1 copy.14.weight
  72.2 4.4 %input_grads.1 = (bf16[4,32,512]{2,1,0:T(8,128)(2,1)}, bf16[4,32,512]{2,1,0:T(8,128)(2,1)}, bf16[4,32,512]{2,1,0:T(8,128)(2,1)}) custom-call(bf16[4,32,512]{2,1,0:T(8,128)(2,1)S(1)} %bitcast.15, bf16[4,32,512]{2,1,0:T(8,128)(2,1)S(1)} %bitcast.17, bf16[4,32,512]{2,1,0:T(8,128)(2,1)S(1)} %bitcast.19, bf16[4,32,512]{2,1,0:T(8,128)(2,1)S(1)} %bitcast.21, ...), custom_call_target="tpu_custom_call" | custom-call | flops 335544320 | bytes 1048576 | tf_op jit(solution)/shard_map/input_grads/pallas_call | solution.py:139
  76.6 0.0 all-to-all-done.4
  76.6 0.1 convert_reduce_fusion
  76.6 5.7 %all-gather = f32[4,4,512]{2,1,0:T(4,128)S(1)} all-gather(f32[2,4,512]{2,1,0:T(4,128)S(1)} %convert_reduce_fusion), channel_id=2, replica_groups=mesh['y'=4,'z'=16,'xh'=2,'xl'=2,'core'=2] {'core'}, dimensions={0}, use_global_device_ids=true | all-gather | bytes 49152 | tf_op jit(solution)/shard_map/all_gather | solution.py:245
  82.4 0.9 %pair_grad.1 = f32[32,4,512]{2,1,0:T(4,128)} custom-call(bf16[32,4]{1,0:T(8,128)(2,1)S(1)} %copy.14.weight, f32[2,2,4,512]{3,2,1,0:T(4,128)S(1)} %bitcast.22), custom_call_target="tpu_custom_call" | custom-call | tf_op jit(solution)/shard_map/pair_grad/pallas_call | solution.py:211
  (5 shorter events, 0.1 us)
Async XLA Ops:
  0.6 0.9 %copy-start = (bf16[32,4,512]{2,1,0:T(4,128)(2,1)S(1)}, bf16[32,4,512]{2,1,0:T(4,128)(2,1)}, u32[]{:S(2)}) copy-start(bf16[32,4,512]{2,1,0:T(4,128)(2,1)} %param.10) | copy-start | bytes 393220
  31.0 13.3 %copy-start.1 = (bf16[1,4,32,512]{3,2,1,0:T(8,128)(2,1)S(1)}, bf16[1,4,32,512]{3,2,1,0:T(8,128)(2,1)}, u32[]{:S(2)}) copy-start(bf16[1,4,32,512]{3,2,1,0:T(8,128)(2,1)} %param.6) | copy-start | bytes 393220
  31.0 13.3 %copy-start.2 = (bf16[1,4,32,512]{3,2,1,0:T(8,128)(2,1)S(1)}, bf16[1,4,32,512]{3,2,1,0:T(8,128)(2,1)}, u32[]{:S(2)}) copy-start(bf16[1,4,32,512]{3,2,1,0:T(8,128)(2,1)} %param.7) | copy-start | bytes 393220
  31.0 13.3 %copy-start.3 = (bf16[1,4,32,512]{3,2,1,0:T(8,128)(2,1)S(1)}, bf16[1,4,32,512]{3,2,1,0:T(8,128)(2,1)}, u32[]{:S(2)}) copy-start(bf16[1,4,32,512]{3,2,1,0:T(8,128)(2,1)} %param.8) | copy-start | bytes 393220
  31.0 13.2 %copy-start.4 = (bf16[1,4,32,512]{3,2,1,0:T(8,128)(2,1)S(1)}, bf16[1,4,32,512]{3,2,1,0:T(8,128)(2,1)}, u32[]{:S(2)}) copy-start(bf16[1,4,32,512]{3,2,1,0:T(8,128)(2,1)} %param.9) | copy-start | bytes 393220
  59.4 12.7 %copy-start.5 = (bf16[32,4]{0,1:T(4,128)(2,1)S(1)}, bf16[32,4]{0,1:T(4,128)(2,1)}, u32[]{:S(2)}) copy-start(bf16[32,4]{0,1:T(4,128)(2,1)} %param.11) | copy-start | bytes 772
  59.4 17.2 %all-to-all-start.4 = ((bf16[32,4,512]{2,1,0:T(4,128)(2,1)}), bf16[32,4,512]{2,1,0:T(4,128)(2,1)S(1)}, u32[]{:S(2)}, u32[]{:S(2)}) async-start(bf16[32,4,512]{2,1,0:T(4,128)(2,1)} %bitcast.5), calls=%async_computation.4 | async-start | bytes 262144 | tf_op jit(solution)/shard_map/all_to_all | solution.py:223

commit v7 on v6

--- a/solution.py
+++ b/solution.py
@@ -12,11 +12,12 @@
 BLK = ("y", "z", "xh")
 HEAD = ("xl", "core")
 PLANE = ("y", "xh")
+FIRST_IN, FIRST_OUT = 10, 10
 PLANE_ORDER = (5, 4, 7, 6, 1, 0, 3, 2)
 
 
-def middle_first(count):
-    return [(i + count // 2) % count for i in range(count)]
+def starting(first, count):
+    return [(first + i) % count for i in range(count)]
 
 
 def place(y, xh):
@@ -48,9 +49,9 @@
     return low.reshape(-1, rows.shape[-1]), high.reshape(-1, rows.shape[-1])
 
 
-def turned(rows):
-    half = rows.shape[0] // 2
-    return jnp.concatenate([rows[half:], rows[:half]], axis=0)
+def rolled(rows, blocks):
+    cut = 8 * blocks % rows.shape[0]
+    return jnp.concatenate([rows[cut:], rows[:cut]], axis=0) if cut else rows
 
 
 def bias_tile(bias, tile):
@@ -58,7 +59,7 @@
         (bias[place(tile, part)].astype(jnp.float32) * LOG2E).reshape(-1, 8, bias.shape[-1])
         for part in range(2)
     )
-    return turned(interleave(low, high))
+    return rolled(interleave(low, high), -FIRST_IN)
 
 
 def softmax_parts(query, keyset, wide):
@@ -85,7 +86,7 @@
             summed = dscores if summed is None else summed + dscores
         for index, tile in enumerate(tiles):
             rows = summed[index * own : (index + 1) * own]
-            for part, half in enumerate(separate(turned(rows))):
+            for part, half in enumerate(separate(rolled(rows, FIRST_OUT))):
                 total[place(tile, part)] = half.astype(jnp.bfloat16)
 
 
@@ -106,9 +107,10 @@
     own = 2 * bias.shape[1]
     scale = DH ** (-0.5)
     for row in range(query.shape[0]):
-        for tile in range(bias.shape[0] // 2):
-            columns = slice(tile * own, (tile + 1) * own)
-            wide = bias_tile(bias, tile)
+        for pair in range(bias.shape[0] // 4):
+            tiles = (2 * pair, 2 * pair + 1)
+            columns = slice(tiles[0] * own, (tiles[1] + 1) * own)
+            wide = jnp.concatenate([bias_tile(bias, tile) for tile in tiles], axis=0)
             weights, inverse = softmax_parts(query[row, :, columns], keyset[row], wide)
             probs = weights * inverse
             low = probs.astype(jnp.bfloat16)
@@ -231,13 +233,13 @@
     partial = jnp.einsum("ch,cjk->hjk", bias_weight, pair_norm, preferred_element_type=jnp.float32)
     own = jnp.sum(exchange(partial, HEAD), axis=0).astype(jnp.bfloat16)
     line = jnp.broadcast_to(own[None], (nz, rows, width))
-    line = exchange(line, "z", middle_first(nz)).reshape(nz * rows, width)
+    line = exchange(line, "z", starting(FIRST_IN, nz)).reshape(nz * rows, width)
     planes = lax.axis_size(PLANE)
     bias = exchange(jnp.broadcast_to(line[None], (planes,) + line.shape), PLANE, PLANE_ORDER)
 
     total = bias_sum(query, keyset, values, cotangent, bias)
     line = fold(exchange(total, PLANE, PLANE_ORDER), rows, 2)
-    order = [2 * z + xl for z in middle_first(nz) for xl in (1, 0)]
+    order = [2 * z + xl for z in starting(FIRST_OUT, nz) for xl in (1, 0)]
     line = exchange(line.reshape(nz * 2, rows, width), ("z", "xl"), order)
     grads = input_grads(query, keyset, values, cotangent, bias)
     line, *grads = lax.optimization_barrier((line, *grads))

time: 83.6 us -> 83.5 us (level)
  starting transfers between devices: 12.7 us -> 10.9 us
  waiting for transfers between devices: 0.01 us -> 1.48 us
    all_to_all x1, starting transfers between devices: 12.7 us -> 10.9 us  [exchange(): lax.all_to_all(blocks, axes, 0, 0, axis_index_groups=groups, tiled=True)]
    all_to_all x1, waiting for transfers between devices: 0.01 us -> 1.48 us  [exchange(): lax.all_to_all(blocks, axes, 0, 0, axis_index_groups=groups, tiled=True)]
  transfers between devices with their start and end apart: 1 -> 1, of which waited for: 0 -> 1; matrix products, arithmetic and copies ran while one was open for 0% -> 0% of each run, Pallas kernels for 5% -> 5%
where the time goes in v7:
time: 83.5 us; the launch traced here: 83.1 us
  blocking collectives  59.4 us (71%)
  starting transfers between devices  10.9 us (13%)
  Pallas kernels  8.53 us (10%)
  waiting for transfers between devices  1.48 us (2%)
  local copies, waits for them, and re-layouts  1.13 us (1%)
    all_to_all x4, blocking collectives, exchange(): lax.all_to_all(blocks, axes, 0, 0, axis_index_groups=groups, tiled=True)  53.4 us
    all_to_all x1, starting transfers between devices, exchange(): lax.all_to_all(blocks, axes, 0, 0, axis_index_groups=groups, tiled=True)  10.9 us
    all_gather x1, blocking collectives, shards(): every_head = lax.all_gather(own, 'core', axis=0)  5.98 us
    pallas_call x1, Pallas kernels, input_grads(): pl.pallas_call(inputs_kernel, grid=(1,), in_specs=[held] * 5, out_specs=[...  4.31 us
    pallas_call x1, Pallas kernels, bias_sum(): pl.pallas_call(sum_kernel, in_specs=[held] * 5, out_specs=held, out_shape...  2.57 us
  transfers between devices with their start and end apart: 1, of which 1 were waited for; matrix products, arithmetic and copies ran while one was open for 0% of the time, Pallas kernels for 5%

profile of v7, /device:TPU:1, one launch (start us, length us, event | category | flops | bytes accessed | tf_op | source)
XLA Modules:
  0.0 83.1 jit_solution(1953094710528508554)
XLA Ops:
  0.6 0.0 copy-start
  0.6 0.9 %copy-done = bf16[32,4,512]{2,1,0:T(4,128)(2,1)S(1)} copy-done((bf16[32,4,512]{2,1,0:T(4,128)(2,1)S(1)}, bf16[32,4,512]{2,1,0:T(4,128)(2,1)}, u32[]{:S(2)}) %copy-start) | copy-done | bytes 131096
  1.5 0.8 fusion
  2.4 12.4 %all_to_all.25 = f32[4,4,512]{2,1,0:T(4,128)S(1)} all-to-all(f32[4,4,512]{2,1,0:T(4,128)S(1)} %copy.13), channel_id=1, replica_groups=mesh['y'=4,'z'=16,'xh'=2,'xl'=2,'core'=2] {'xl','core'}, dimensions={0} | all-to-all | bytes 65536 | tf_op jit(solution)/shard_map/all_to_all | solution.py:225
  14.8 16.0 %all_to_all.26 = bf16[16,4,512]{2,1,0:T(4,128)(2,1)S(1)} all-to-all(bf16[16,4,512]{2,1,0:T(4,128)(2,1)S(1)} %broadcast_in_dim.22), channel_id=1, replica_groups={{80,88,96,104,112,120,0,8,16,24,32,40,48,56,64,72},{81,89,97,105,113,12..., dimensions={0} | all-to-all | bytes 131072 | tf_op jit(solution)/shard_map/all_to_all | solution.py:225
  30.9 0.0 copy-start.1
  30.9 0.0 copy-start.2
  30.9 0.0 copy-start.3
  30.9 0.0 copy-start.4
  31.0 13.2 %all_to_all.27.bias = bf16[8,64,512]{2,1,0:T(8,128)(2,1)S(1)} all-to-all(bf16[8,64,512]{2,1,0:T(8,128)(2,1)S(1)} %broadcast_in_dim.24), channel_id=1, replica_groups={{260,256,388,384,4,0,132,128},{261,257,389,385,5,1,133,129},{262,258,39..., dimensions={0} | all-to-all | bytes 1048576 | tf_op jit(solution)/shard_map/all_to_all | solution.py:225
  44.2 0.0 copy-done.1
  44.2 0.0 copy-done.2
  44.2 0.0 copy-done.3
  44.2 0.0 copy-done.4
  44.2 2.6 %bias_sum.1 = bf16[8,64,512]{2,1,0:T(8,128)(2,1)S(1)} custom-call(bf16[4,32,512]{2,1,0:T(8,128)(2,1)S(1)} %bitcast.14, bf16[4,32,512]{2,1,0:T(8,128)(2,1)S(1)} %bitcast.16, bf16[4,32,512]{2,1,0:T(8,128)(2,1)S(1)} %bitcast.18, bf16[4,32,512]{2,1,0:T(8,128)(2,1)S(1)} %bitcast.20, bf16[8,64,512]{2,1,0:T(8,128)(2,1)S(1)} %all_to_all.27.bias), custom_call_target="tpu_custom_call" | custom-call | tf_op jit(solution)/shard_map/bias_sum/pallas_call | solution.py:95
  46.8 11.8 %all_to_all.28.parts = bf16[8,64,512]{2,1,0:T(8,128)(2,1)S(1)} all-to-all(bf16[8,64,512]{2,1,0:T(8,128)(2,1)S(1)} %bias_sum.1), channel_id=1, replica_groups={{260,256,388,384,4,0,132,128},{261,257,389,385,5,1,133,129},{262,258,39..., dimensions={0} | all-to-all | bytes 1048576 | tf_op jit(solution)/shard_map/all_to_all | solution.py:225
  58.6 0.7 fold.1
  59.3 0.0 copy-start.5
  59.3 10.9 %all-to-all-start.4 = ((bf16[32,4,512]{2,1,0:T(4,128)(2,1)}), bf16[32,4,512]{2,1,0:T(4,128)(2,1)S(1)}, u32[]{:S(2)}, u32[]{:S(2)}) async-start(bf16[32,4,512]{2,1,0:T(4,128)(2,1)} %bitcast.5), calls=%async_computation.4 | async-start | bytes 262144 | tf_op jit(solution)/shard_map/all_to_all | solution.py:225
  70.2 0.0 copy-done.5
  70.2 0.1 copy.14.weight
  70.3 4.3 %input_grads.1 = (bf16[4,32,512]{2,1,0:T(8,128)(2,1)}, bf16[4,32,512]{2,1,0:T(8,128)(2,1)}, bf16[4,32,512]{2,1,0:T(8,128)(2,1)}) custom-call(bf16[4,32,512]{2,1,0:T(8,128)(2,1)S(1)} %bitcast.15, bf16[4,32,512]{2,1,0:T(8,128)(2,1)S(1)} %bitcast.17, bf16[4,32,512]{2,1,0:T(8,128)(2,1)S(1)} %bitcast.19, bf16[4,32,512]{2,1,0:T(8,128)(2,1)S(1)} %bitcast.21, ...), custom_call_target="tpu_custom_call" | custom-call | flops 335544320 | bytes 1048576 | tf_op jit(solution)/shard_map/input_grads/pallas_call | solution.py:141
  74.7 1.5 %all-to-all-done.4 = bf16[32,4,512]{2,1,0:T(4,128)(2,1)S(1)} async-done(((bf16[32,4,512]{2,1,0:T(4,128)(2,1)}), bf16[32,4,512]{2,1,0:T(4,128)(2,1)S(1)}, u32[]{:S(2)}, u32[]{:S(2)}) %all-to-all-start.4) | async-done | bytes 131104 | tf_op jit(solution)/shard_map/all_to_all | solution.py:225
  76.1 0.1 convert_reduce_fusion
  76.2 6.0 %all-gather = f32[4,4,512]{2,1,0:T(4,128)S(1)} all-gather(f32[2,4,512]{2,1,0:T(4,128)S(1)} %convert_reduce_fusion), channel_id=2, replica_groups=mesh['y'=4,'z'=16,'xh'=2,'xl'=2,'core'=2] {'core'}, dimensions={0}, use_global_device_ids=true | all-gather | bytes 49152 | tf_op jit(solution)/shard_map/all_gather | solution.py:247
  82.2 0.9 %pair_grad.1 = f32[32,4,512]{2,1,0:T(4,128)} custom-call(bf16[32,4]{1,0:T(8,128)(2,1)S(1)} %copy.14.weight, f32[2,2,4,512]{3,2,1,0:T(4,128)S(1)} %bitcast.22), custom_call_target="tpu_custom_call" | custom-call | tf_op jit(solution)/shard_map/pair_grad/pallas_call | solution.py:213
  (5 shorter events, 0.1 us)
Async XLA Ops:
  0.6 0.9 %copy-start = (bf16[32,4,512]{2,1,0:T(4,128)(2,1)S(1)}, bf16[32,4,512]{2,1,0:T(4,128)(2,1)}, u32[]{:S(2)}) copy-start(bf16[32,4,512]{2,1,0:T(4,128)(2,1)} %param.10) | copy-start | bytes 393220
  30.9 13.2 %copy-start.1 = (bf16[1,4,32,512]{3,2,1,0:T(8,128)(2,1)S(1)}, bf16[1,4,32,512]{3,2,1,0:T(8,128)(2,1)}, u32[]{:S(2)}) copy-start(bf16[1,4,32,512]{3,2,1,0:T(8,128)(2,1)} %param.6) | copy-start | bytes 393220
  30.9 13.2 %copy-start.2 = (bf16[1,4,32,512]{3,2,1,0:T(8,128)(2,1)S(1)}, bf16[1,4,32,512]{3,2,1,0:T(8,128)(2,1)}, u32[]{:S(2)}) copy-start(bf16[1,4,32,512]{3,2,1,0:T(8,128)(2,1)} %param.7) | copy-start | bytes 393220
  30.9 13.2 %copy-start.3 = (bf16[1,4,32,512]{3,2,1,0:T(8,128)(2,1)S(1)}, bf16[1,4,32,512]{3,2,1,0:T(8,128)(2,1)}, u32[]{:S(2)}) copy-start(bf16[1,4,32,512]{3,2,1,0:T(8,128)(2,1)} %param.8) | copy-start | bytes 393220
  30.9 13.2 %copy-start.4 = (bf16[1,4,32,512]{3,2,1,0:T(8,128)(2,1)S(1)}, bf16[1,4,32,512]{3,2,1,0:T(8,128)(2,1)}, u32[]{:S(2)}) copy-start(bf16[1,4,32,512]{3,2,1,0:T(8,128)(2,1)} %param.9) | copy-start | bytes 393220
  59.3 10.9 %copy-start.5 = (bf16[32,4]{0,1:T(4,128)(2,1)S(1)}, bf16[32,4]{0,1:T(4,128)(2,1)}, u32[]{:S(2)}) copy-start(bf16[32,4]{0,1:T(4,128)(2,1)} %param.11) | copy-start | bytes 772
  59.3 16.8 %all-to-all-start.4 = ((bf16[32,4,512]{2,1,0:T(4,128)(2,1)}), bf16[32,4,512]{2,1,0:T(4,128)(2,1)S(1)}, u32[]{:S(2)}, u32[]{:S(2)}) async-start(bf16[32,4,512]{2,1,0:T(4,128)(2,1)} %bitcast.5), calls=%async_computation.4 | async-start | bytes 262144 | tf_op jit(solution)/shard_map/all_to_all | solution.py:225

commit v8 on v7

--- a/solution.py
+++ b/solution.py
@@ -12,7 +12,7 @@
 BLK = ("y", "z", "xh")
 HEAD = ("xl", "core")
 PLANE = ("y", "xh")
-FIRST_IN, FIRST_OUT = 10, 10
+FIRST_IN, FIRST_OUT = 10, 8
 PLANE_ORDER = (5, 4, 7, 6, 1, 0, 3, 2)
 
 

time: 83.5 us -> 83.5 us (level)
  starting transfers between devices: 10.9 us -> 12.6 us
  waiting for transfers between devices: 1.48 us -> 0.01 us
    all_to_all x1, starting transfers between devices: 10.9 us -> 12.6 us  [exchange(): lax.all_to_all(blocks, axes, 0, 0, axis_index_groups=groups, tiled=True)]
    all_to_all x1, waiting for transfers between devices: 1.48 us -> 0.01 us  [exchange(): lax.all_to_all(blocks, axes, 0, 0, axis_index_groups=groups, tiled=True)]
  transfers between devices with their start and end apart: 1 -> 1, of which waited for: 1 -> 0; matrix products, arithmetic and copies ran while one was open for 0% -> 0% of each run, Pallas kernels for 5% -> 5%
where the time goes in v8:
time: 83.5 us; the launch traced here: 83.2 us
  blocking collectives  59.2 us (71%)
  starting transfers between devices  12.6 us (15%)
  Pallas kernels  8.53 us (10%)
  local copies, waits for them, and re-layouts  1.13 us (1%)
    all_to_all x4, blocking collectives, exchange(): lax.all_to_all(blocks, axes, 0, 0, axis_index_groups=groups, tiled=True)  53.4 us
    all_to_all x1, starting transfers between devices, exchange(): lax.all_to_all(blocks, axes, 0, 0, axis_index_groups=groups, tiled=True)  12.6 us
    all_gather x1, blocking collectives, shards(): every_head = lax.all_gather(own, 'core', axis=0)  5.79 us
    pallas_call x1, Pallas kernels, input_grads(): pl.pallas_call(inputs_kernel, grid=(1,), in_specs=[held] * 5, out_specs=[...  4.31 us
    pallas_call x1, Pallas kernels, bias_sum(): pl.pallas_call(sum_kernel, in_specs=[held] * 5, out_specs=held, out_shape...  2.57 us
  transfers between devices with their start and end apart: 1, of which 0 were waited for; matrix products, arithmetic and copies ran while one was open for 0% of the time, Pallas kernels for 5%

profile of v8, /device:TPU:1, one launch (start us, length us, event | category | flops | bytes accessed | tf_op | source)
XLA Modules:
  0.0 83.2 jit_solution(14019241529192958617)
XLA Ops:
  0.6 0.0 copy-start
  0.6 0.9 %copy-done = bf16[32,4,512]{2,1,0:T(4,128)(2,1)S(1)} copy-done((bf16[32,4,512]{2,1,0:T(4,128)(2,1)S(1)}, bf16[32,4,512]{2,1,0:T(4,128)(2,1)}, u32[]{:S(2)}) %copy-start) | copy-done | bytes 131096
  1.5 0.8 fusion
  2.4 12.4 %all_to_all.25 = f32[4,4,512]{2,1,0:T(4,128)S(1)} all-to-all(f32[4,4,512]{2,1,0:T(4,128)S(1)} %copy.13), channel_id=1, replica_groups=mesh['y'=4,'z'=16,'xh'=2,'xl'=2,'core'=2] {'xl','core'}, dimensions={0} | all-to-all | bytes 65536 | tf_op jit(solution)/shard_map/all_to_all | solution.py:225
  14.8 16.0 %all_to_all.26 = bf16[16,4,512]{2,1,0:T(4,128)(2,1)S(1)} all-to-all(bf16[16,4,512]{2,1,0:T(4,128)(2,1)S(1)} %broadcast_in_dim.22), channel_id=1, replica_groups={{80,88,96,104,112,120,0,8,16,24,32,40,48,56,64,72},{81,89,97,105,113,12..., dimensions={0} | all-to-all | bytes 131072 | tf_op jit(solution)/shard_map/all_to_all | solution.py:225
  30.9 0.0 copy-start.1
  30.9 0.0 copy-start.2
  30.9 0.0 copy-start.3
  30.9 0.0 copy-start.4
  31.0 13.2 %all_to_all.27.bias = bf16[8,64,512]{2,1,0:T(8,128)(2,1)S(1)} all-to-all(bf16[8,64,512]{2,1,0:T(8,128)(2,1)S(1)} %broadcast_in_dim.24), channel_id=1, replica_groups={{260,256,388,384,4,0,132,128},{261,257,389,385,5,1,133,129},{262,258,39..., dimensions={0} | all-to-all | bytes 1048576 | tf_op jit(solution)/shard_map/all_to_all | solution.py:225
  44.2 0.0 copy-done.1
  44.2 0.0 copy-done.2
  44.2 0.0 copy-done.3
  44.2 0.0 copy-done.4
  44.2 2.6 %bias_sum.1 = bf16[8,64,512]{2,1,0:T(8,128)(2,1)S(1)} custom-call(bf16[4,32,512]{2,1,0:T(8,128)(2,1)S(1)} %bitcast.14, bf16[4,32,512]{2,1,0:T(8,128)(2,1)S(1)} %bitcast.16, bf16[4,32,512]{2,1,0:T(8,128)(2,1)S(1)} %bitcast.18, bf16[4,32,512]{2,1,0:T(8,128)(2,1)S(1)} %bitcast.20, bf16[8,64,512]{2,1,0:T(8,128)(2,1)S(1)} %all_to_all.27.bias), custom_call_target="tpu_custom_call" | custom-call | tf_op jit(solution)/shard_map/bias_sum/pallas_call | solution.py:95
  46.8 11.8 %all_to_all.28.parts = bf16[8,64,512]{2,1,0:T(8,128)(2,1)S(1)} all-to-all(bf16[8,64,512]{2,1,0:T(8,128)(2,1)S(1)} %bias_sum.1), channel_id=1, replica_groups={{260,256,388,384,4,0,132,128},{261,257,389,385,5,1,133,129},{262,258,39..., dimensions={0} | all-to-all | bytes 1048576 | tf_op jit(solution)/shard_map/all_to_all | solution.py:225
  58.6 0.7 fold.1
  59.3 0.0 copy-start.5
  59.3 12.6 %all-to-all-start.4 = ((bf16[32,4,512]{2,1,0:T(4,128)(2,1)}), bf16[32,4,512]{2,1,0:T(4,128)(2,1)S(1)}, u32[]{:S(2)}, u32[]{:S(2)}) async-start(bf16[32,4,512]{2,1,0:T(4,128)(2,1)} %bitcast.5), calls=%async_computation.4 | async-start | bytes 262144 | tf_op jit(solution)/shard_map/all_to_all | solution.py:225
  72.0 0.0 copy-done.5
  72.0 0.1 copy.14.weight
  72.1 4.3 %input_grads.1 = (bf16[4,32,512]{2,1,0:T(8,128)(2,1)}, bf16[4,32,512]{2,1,0:T(8,128)(2,1)}, bf16[4,32,512]{2,1,0:T(8,128)(2,1)}) custom-call(bf16[4,32,512]{2,1,0:T(8,128)(2,1)S(1)} %bitcast.15, bf16[4,32,512]{2,1,0:T(8,128)(2,1)S(1)} %bitcast.17, bf16[4,32,512]{2,1,0:T(8,128)(2,1)S(1)} %bitcast.19, bf16[4,32,512]{2,1,0:T(8,128)(2,1)S(1)} %bitcast.21, ...), custom_call_target="tpu_custom_call" | custom-call | flops 335544320 | bytes 1048576 | tf_op jit(solution)/shard_map/input_grads/pallas_call | solution.py:141
  76.4 0.0 all-to-all-done.4
  76.4 0.1 convert_reduce_fusion
  76.5 5.8 %all-gather = f32[4,4,512]{2,1,0:T(4,128)S(1)} all-gather(f32[2,4,512]{2,1,0:T(4,128)S(1)} %convert_reduce_fusion), channel_id=2, replica_groups=mesh['y'=4,'z'=16,'xh'=2,'xl'=2,'core'=2] {'core'}, dimensions={0}, use_global_device_ids=true | all-gather | bytes 49152 | tf_op jit(solution)/shard_map/all_gather | solution.py:247
  82.3 0.9 %pair_grad.1 = f32[32,4,512]{2,1,0:T(4,128)} custom-call(bf16[32,4]{1,0:T(8,128)(2,1)S(1)} %copy.14.weight, f32[2,2,4,512]{3,2,1,0:T(4,128)S(1)} %bitcast.22), custom_call_target="tpu_custom_call" | custom-call | tf_op jit(solution)/shard_map/pair_grad/pallas_call | solution.py:213
  (5 shorter events, 0.1 us)
Async XLA Ops:
  0.6 0.9 %copy-start = (bf16[32,4,512]{2,1,0:T(4,128)(2,1)S(1)}, bf16[32,4,512]{2,1,0:T(4,128)(2,1)}, u32[]{:S(2)}) copy-start(bf16[32,4,512]{2,1,0:T(4,128)(2,1)} %param.10) | copy-start | bytes 393220
  30.9 13.2 %copy-start.1 = (bf16[1,4,32,512]{3,2,1,0:T(8,128)(2,1)S(1)}, bf16[1,4,32,512]{3,2,1,0:T(8,128)(2,1)}, u32[]{:S(2)}) copy-start(bf16[1,4,32,512]{3,2,1,0:T(8,128)(2,1)} %param.6) | copy-start | bytes 393220
  30.9 13.2 %copy-start.2 = (bf16[1,4,32,512]{3,2,1,0:T(8,128)(2,1)S(1)}, bf16[1,4,32,512]{3,2,1,0:T(8,128)(2,1)}, u32[]{:S(2)}) copy-start(bf16[1,4,32,512]{3,2,1,0:T(8,128)(2,1)} %param.7) | copy-start | bytes 393220
  30.9 13.2 %copy-start.3 = (bf16[1,4,32,512]{3,2,1,0:T(8,128)(2,1)S(1)}, bf16[1,4,32,512]{3,2,1,0:T(8,128)(2,1)}, u32[]{:S(2)}) copy-start(bf16[1,4,32,512]{3,2,1,0:T(8,128)(2,1)} %param.8) | copy-start | bytes 393220
  30.9 13.2 %copy-start.4 = (bf16[1,4,32,512]{3,2,1,0:T(8,128)(2,1)S(1)}, bf16[1,4,32,512]{3,2,1,0:T(8,128)(2,1)}, u32[]{:S(2)}) copy-start(bf16[1,4,32,512]{3,2,1,0:T(8,128)(2,1)} %param.9) | copy-start | bytes 393220
  59.3 12.7 %copy-start.5 = (bf16[32,4]{0,1:T(4,128)(2,1)S(1)}, bf16[32,4]{0,1:T(4,128)(2,1)}, u32[]{:S(2)}) copy-start(bf16[32,4]{0,1:T(4,128)(2,1)} %param.11) | copy-start | bytes 772
  59.3 17.1 %all-to-all-start.4 = ((bf16[32,4,512]{2,1,0:T(4,128)(2,1)}), bf16[32,4,512]{2,1,0:T(4,128)(2,1)S(1)}, u32[]{:S(2)}, u32[]{:S(2)}) async-start(bf16[32,4,512]{2,1,0:T(4,128)(2,1)} %bitcast.5), calls=%async_computation.4 | async-start | bytes 262144 | tf_op jit(solution)/shard_map/all_to_all | solution.py:225
